TPU v7x, 128 devices: a whole 4x4x4 slice. The times are simulated.
128 devices in a mesh: tile: 32 (over y, z, core), grp: 4 (over x).
Axes of the slice: x: 4, y: 4, z: 4, core: 2. Of those that a mesh axis runs over, the one named last changes fastest.
Arguments:
- flood_state: float32 [4, 128, 3, 256, 256], P('grp', 'tile'), may hold values from -1.6 to 3.5, as said below
- terrain: float32 [4, 128, 2, 256, 256], P('grp', 'tile'), may hold values from 0 to 1.5, as said below
- destination: int32 [4, 128], P('grp'), may hold values from 0 to 127, as said below
- wet_mask: int32 [4, 128], P('grp', 'tile'), may hold values from 0 to 1, as said below
- neighbours: int32 [4, 128, 4], P('grp', 'tile'), may hold values from -1 to 7, as said below
- inflow_cells: int32 [4, 128, 16], P('grp', 'tile'), may hold values from 0 to 65535
- inflow_rates: float32 [4, 128, 16], P('grp', 'tile'), may hold values from 1 to 50
Outputs:
- new_state: float32 [4, 128, 3, 256, 256], P('grp', 'tile')
Inputs may be any that keep to these rules, and one draw needn't show every extreme that they name: `flood_state`: field 0 is the water depth, 1.5 to 3.5; fields 1 and 2 the unit discharges. `terrain`: field 0 is the bed elevation, 0 to 1.5; field 1 the Manning coefficient, 0.03 to 0.3. `destination`: in each band a permutation of the positions; the 4 blocks of device t (positions t * 4 to t * 4 + 3) go to the devices (t + k) modulo 32 of the same band for k = 0 to 3, one block to each. `wet_mask`: a dry block has only -1 entries and no entry names it. `neighbours`: entries follow the encoding of the steps, from -1 to 7, and are mutual: if a block names another on one side, that one names it on the opposite side.
All inputs are finite; a program needn't handle non-finite values.
Results may differ from a plain program's by a relative error of at most 0.00002.
Values sent between devices are 32-bit elements; how exact they have to be, the bound alone decides.
No kernel may reach another device: no remote copies, remote signals or barrier semaphores. Data moves between devices by JAX's collectives and lax.ppermute only.
A program may use at most 64 MiB of HBM per device.

v0:
```python
import functools

import jax
import jax.numpy as jnp
from jax import lax
from jax.experimental import pallas as pl
from jax.experimental.pallas import tpu as pltpu
from jax.sharding import PartitionSpec as P

F32 = jnp.float32
GRAVITY = 9.81
SPACING = 10.0
TIMESTEP = 0.2
CENTRE_WEIGHT = 0.7
DEPTH_FLOOR = 0.1
SIDE = 256
HALF = 128
BLOCKS = 4
RIVERS = 16
ROWS = 64
GAIN = TIMESTEP / (SPACING * SPACING)
RATIO = TIMESTEP / SPACING

ANY = pl.BlockSpec(memory_space=pl.ANY)
VMEM = pl.BlockSpec(memory_space=pltpu.VMEM)
SMEM = pl.BlockSpec(memory_space=pltpu.SMEM)
HBM = pl.BlockSpec(memory_space=pltpu.HBM)
RING = 4
CUT = 64
OWN_SHIFTS = (0, 0)
A_SHIFTS = (2, 2)
W_SHIFTS = (3, 1)
X_SHIFTS = (1, 3)


def shape(*dims):
    return jax.ShapeDtypeStruct(dims, F32)


def cost(flops, bytes_accessed):
    return pl.CostEstimate(flops=flops, bytes_accessed=bytes_accessed, transcendentals=0)


def face(eta_l, eta_r, z_l, z_r, rough, flow_left, flow_mid, flow_right):
    depth = jnp.maximum(eta_l, eta_r) - jnp.maximum(z_l, z_r)
    floored = jnp.maximum(depth, DEPTH_FLOOR)
    blended = CENTRE_WEIGHT * flow_mid + 0.5 * (1.0 - CENTRE_WEIGHT) * (flow_left + flow_right)
    slope = (GRAVITY * TIMESTEP / SPACING) * depth * (eta_r - eta_l)
    friction = 1.0 + (GRAVITY * TIMESTEP) * rough * rough * jnp.abs(flow_mid) * jnp.exp(
        (-7.0 / 3.0) * jnp.log(floored)
    )
    return (blended - slope) / friction


def core():
    return lax.rem(lax.axis_index("tile"), 2)


def params(mib):
    return pltpu.CompilerParams(vmem_limit_bytes=mib << 20)


def tile_offset(dest_ref, tile, slot):
    tiles = lax.axis_size("tile")
    return lax.rem(lax.div(dest_ref[0, tile * BLOCKS + slot], BLOCKS) - tile + tiles, tiles)


def leaving_slot(dest_ref, shift):
    me = lax.axis_index("tile")
    slot = jnp.int32(0)
    for j in range(1, BLOCKS):
        slot = jnp.where(tile_offset(dest_ref, me, j) == shift, j, slot)
    return slot


def landing_slot(dest_ref, shift, back=0):
    tiles = lax.axis_size("tile")
    sender = lax.rem(lax.axis_index("tile") - shift - back + 2 * tiles, tiles)
    slot = jnp.int32(0)
    for j in range(BLOCKS):
        place = lax.rem(dest_ref[0, sender * BLOCKS + j], BLOCKS)
        slot = jnp.where(tile_offset(dest_ref, sender, j) == shift, place, slot)
    return slot


def lanes(rows, columns):
    return lax.broadcasted_iota(jnp.int32, (rows, columns), 1)


def in_hbm(x):
    return pltpu.with_memory_space_constraint(x, pltpu.HBM)


def pick_kernel(dest, state, a_low, a_high, sems):
    slot = leaving_slot(dest, 2)
    parts = (
        (state.at[0, slot, :, pl.ds(0, CUT)], a_low),
        (state.at[0, slot, :, pl.ds(CUT, SIDE - CUT)], a_high),
    )
    loads = [pltpu.make_async_copy(part, ref, sems.at[i]) for i, (part, ref) in enumerate(parts)]
    for load in loads:
        load.start()
    for load in loads:
        load.wait()


def pick_early(dest, state):
    return pl.pallas_call(
        pick_kernel,
        out_shape=[shape(3, CUT, SIDE), shape(3, SIDE - CUT, SIDE)],
        in_specs=[SMEM, HBM],
        out_specs=[VMEM] * 2,
        scratch_shapes=[pltpu.SemaphoreType.DMA((2,))],
        compiler_params=params(4),
        cost_estimate=cost(0, 0),
    )(dest, state)


def prepare_kernel(
    dest, entries, state, a_low, a_high, ground_in, cells, rates,
    own, block_w, block_x, low, high, pack0, pack1, pack2, pack3, pack4, pack_back, terrain, sems,
):
    slots = [leaving_slot(dest, k) for k in range(BLOCKS)]
    first_core = core() == 0
    slot_w = jnp.where(first_core, slots[1], slots[3])
    slot_x = jnp.where(first_core, slots[3], slots[1])
    held = (block_w, block_x, own)
    loads = [pltpu.make_async_copy(ground_in, terrain, sems.at[3])]
    for i, (slot, ref) in enumerate(zip((slot_w, slot_x, slots[0]), held)):
        loads.append(pltpu.make_async_copy(state.at[0, slot], ref, sems.at[i]))
    for load in loads:
        load.start()
    lane = lanes(SIDE, HALF)

    def strips(parts, write):
        ref, tail = parts[0], parts[-1]
        size = tail.shape[1]

        def half(columns):
            return [jnp.concatenate([part[f, :, columns] for part in parts]) for f in range(3)]

        west = half(slice(0, HALF))
        east = half(slice(HALF, SIDE))
        packed = jnp.where(lane < 3, west[0], pltpu.roll(west[1], 3, 1))
        packed = jnp.where(lane < 6, packed, pltpu.roll(west[2], 6, 1))
        packed = jnp.where(lane < 8, packed, pltpu.roll(east[0], 10, 1))
        packed = jnp.where(lane < 10, packed, pltpu.roll(east[1], 13, 1))
        packed = jnp.where(lane < 13, packed, pltpu.roll(east[2], 14, 1))
        turned = packed.T
        south = jnp.concatenate([ref[0, 0:3], ref[2, 0:3], ref[1, 0:2]])
        north = jnp.concatenate(
            [tail[0, size - 2 : size], tail[2, size - 3 : size], tail[1, size - 1 : size], jnp.zeros((2, SIDE), F32)]
        )
        write(turned[0:8], south, turned[8:16], north)

    strip_out = (pack0, pack1, pack2, pack3)
    west_out = (pack_back.at[0], pack0.at[4], pack1.at[5], pack2.at[5])
    east_out = (pack1.at[4], pack2.at[4], pack3.at[4], pack4.at[0])

    def write(k, west, south, east, north):
        for i, value in enumerate((west, south, east, north)):
            strip_out[k][i] = value
        east_out[k][...] = east
        west_out[k][...] = west

    def write_by_core(first, second):
        def both(*values):
            pl.when(first_core)(lambda: write(first, *values))
            pl.when(jnp.logical_not(first_core))(lambda: write(second, *values))

        return both

    strips((a_low, a_high), functools.partial(write, 2))
    along = lanes(BLOCKS, SIDE)
    spills = [jnp.zeros((BLOCKS, SIDE), F32) for _ in range(2)]
    for p in range(RIVERS):
        cell = cells[0, :, p : p + 1] - along * SIDE
        rate = GAIN * rates[0, :, p : p + 1]
        for i, place in enumerate((0, SIDE - 1)):
            spills[i] = spills[i] + jnp.where(cell == place, rate, 0.0)
    loads[0].wait()
    for b in range(BLOCKS):
        west = [terrain[0, b, f, :, :HALF] for f in range(2)]
        east = [terrain[0, b, f, :, HALF:] for f in range(2)]
        packed = jnp.where(lane < 3, west[0], pltpu.roll(west[1], 3, 1))
        packed = jnp.where(lane < 5, packed, pltpu.roll(east[0], 7, 1))
        packed = jnp.where(lane < 7, packed, pltpu.roll(east[1], 9, 1))
        turned = packed.T
        for q in range(5):
            low[q, b : b + 1] = turned[q : q + 1]
        for q in range(4):
            high[q, b : b + 1] = turned[5 + q : 6 + q]
        for q in range(3):
            low[q, 4 + b : 5 + b] = terrain[0, b, 0, q : q + 1]
        for q in range(2):
            low[3 + q, 4 + b : 5 + b] = terrain[0, b, 1, q : q + 1]
            high[q, 4 + b : 5 + b] = terrain[0, b, 0, SIDE - 2 + q : SIDE - 1 + q]
            high[2 + q, 4 + b : 5 + b] = terrain[0, b, 1, SIDE - 2 + q : SIDE - 1 + q]
    for b in range(BLOCKS):
        line = slice(b, b + 1)
        links = [jnp.full((1, SIDE), entries[0, b, side].astype(F32), F32) for side in (2, 3)]
        blank = [jnp.zeros((1, SIDE), F32)]
        pack1[6 + b] = jnp.concatenate([high[q, line] for q in range(4)] + [spills[1][line]] + links + blank)
        pack_back[1 + b] = jnp.concatenate(
            [low[0, line], low[1, line], low[3, line], spills[0][line]] + links + blank * 2
        )
    writers = (write_by_core(1, 3), write_by_core(3, 1), functools.partial(write, 0))
    for load, ref, write_out in zip(loads[1:], held, writers):
        load.wait()
        strips((ref,), write_out)


def prepare(dest, entries, state, a_low, a_high, terrain, cells, rates):
    packs = [shape(count, 8, SIDE) for count in (5, 10, 6, 5, 1, 5)]
    return pl.pallas_call(
        prepare_kernel,
        out_shape=[shape(3, SIDE, SIDE)] * 3 + [shape(5, 8, SIDE), shape(4, 8, SIDE)] + packs,
        in_specs=[SMEM, SMEM, HBM, VMEM, VMEM, HBM, VMEM, VMEM],
        out_specs=[VMEM] * 11,
        scratch_shapes=[
            pltpu.VMEM((1, BLOCKS, 2, SIDE, SIDE), F32),
            pltpu.SemaphoreType.DMA((BLOCKS,)),
        ],
        compiler_params=params(12),
        cost_estimate=cost(0, 0),
    )(dest, entries, state, a_low, a_high, terrain, cells, rates)


def gate_kernel(count, *refs):
    del count, refs


def gate(values, keys):
    count = len(values)
    return pl.pallas_call(
        functools.partial(gate_kernel, count),
        out_shape=[jax.ShapeDtypeStruct(v.shape, v.dtype) for v in values],
        in_specs=[ANY] * (count + len(keys)),
        out_specs=[ANY] * count,
        input_output_aliases={i: i for i in range(count)},
        compiler_params=params(1),
        cost_estimate=cost(0, 0),
    )(*values, *keys)


def sides_swapped(x):
    return pltpu.roll(x, 4, 0)


def column(x, at):
    return x[:, at : at + 1]


def put_rim(entry, sub, near_state, near_fixed, far_state, far_fixed, wide, has):
    near = jnp.clip(entry, 0, BLOCKS - 1)
    far = jnp.clip(entry - BLOCKS, 0, BLOCKS - 1)
    alive = entry >= 0
    for i, (close, distant) in enumerate(((near_state, far_state), (near_fixed, far_fixed))):
        rows = jnp.where(entry >= BLOCKS, distant(far), close(near))
        rows = jnp.where(alive, rows, 0.0)
        for q in range(8):
            wide[8 * i + q, sub : sub + 1] = rows[q : q + 1]
    has[sub : sub + 1] = jnp.full((1, SIDE), jnp.where(alive, 1.0, 0.0), F32)


def faces_low(low, ground_low, wide):
    h0, h1, h2, q0, q1, q2 = (low[q] for q in range(6))
    z0, z1, z2, n0, n1 = (ground_low[q] for q in range(5))
    hm, qmm, qm, zm, nm = (wide[q] for q in (1, 3, 4, 9, 11))
    return (
        face(hm + zm, h0 + z0, zm, z0, nm, qmm, qm, q0),
        face(h0 + z0, h1 + z1, z0, z1, n0, qm, q0, q1),
        face(h1 + z1, h2 + z2, z1, z2, n1, q0, q1, q2),
    )


def faces_high(high, ground_high, wide):
    hy, hz, qx, qy, qz = (high[q] for q in range(5))
    zy, zz, ny, nz = (ground_high[q] for q in range(4))
    hp, qp, zp = (wide[q] for q in (0, 3, 8))
    return (
        face(hy + zy, hz + zz, zy, zz, ny, qx, qy, qz),
        face(hz + zz, hp + zp, zz, zp, nz, qy, qz, qp),
    )


def arrange_kernel(
    dest, entries, pack0, pack1, pack2, pack3, pack4, pack_back, ground_low, ground_high, edge_spill,
    low, high, wide_low, wide_high, has_low, has_high, far_east, far_west, to_south, to_north,
    west, east,
):
    for out in (low, high, wide_low, wide_high, has_low, has_high):
        out[...] = jnp.zeros_like(out)
    strips = (pack0, pack1, pack2, pack3)
    west_in = (pack_back.at[0], pack0.at[4], pack1.at[5], pack2.at[5])
    east_in = (pack1.at[4], pack2.at[4], pack3.at[4], pack4.at[0])
    for k in range(BLOCKS):
        strip = strips[k]
        slot = landing_slot(dest, k)
        for side in range(2):
            row = pl.ds(side * 4 + slot, 1)
            for q in range(8):
                low[q, row] = strip[side, q : q + 1]
            for q in range(6):
                high[q, row] = strip[2 + side, q : q + 1]
        for i, out in enumerate((west, to_south, east, to_north)):
            out[slot] = strip[i]
        slot = landing_slot(dest, k, 1)
        far_east[slot] = east_in[k][...]
        slot = landing_slot(dest, k, -1)
        far_west[slot] = west_in[k][...]

    def fixed_low(slot):
        row = pl.ds(slot, 1)
        rows = [ground_low[0, row], ground_low[1, row], ground_low[3, row]]
        return jnp.concatenate(rows + [jnp.zeros((5, SIDE), F32)])

    def fixed_high(slot):
        row = pl.ds(slot, 1)
        return jnp.concatenate([ground_high[q, row] for q in range(4)] + [jnp.zeros((4, SIDE), F32)])

    for b in range(BLOCKS):
        put_rim(
            entries[0, b, 0], b, lambda s: east[s], fixed_high,
            lambda s: far_east[s], lambda s: pack1[6 + s], wide_low, has_low,
        )
        put_rim(
            entries[0, b, 1], b, lambda s: west[s], fixed_low,
            lambda s: far_west[s], lambda s: pack_back[1 + s], wide_high, has_high,
        )
    face_m, face_0, _ = faces_low(low, ground_low, wide_low)
    _, face_z = faces_high(high, ground_high, wide_high)
    face_m = face_m * has_low[...]
    face_z = face_z * has_high[...]
    for b in range(BLOCKS):
        sub = slice(4 + b, 5 + b)
        beside = [f[b : b + 1] for f in (face_m, face_0, face_z)]
        blank = [jnp.zeros((1, SIDE), F32)]
        to_north[4 + b] = jnp.concatenate([ground_high[q, sub] for q in range(4)] + [edge_spill[2, sub]] + beside)
        to_south[4 + b] = jnp.concatenate(
            [ground_low[0, sub], ground_low[1, sub], ground_low[3, sub], edge_spill[0, sub]] + beside + blank
        )
        passed = jnp.concatenate(
            [
                far_east[b, 1:2], far_east[b, 5:6], pack1[6 + b, 1:2], pack1[6 + b, 3:4],
                far_west[b, 0:1], far_west[b, 6:7], pack_back[1 + b, 0:1], pack_back[1 + b, 2:3],
            ]
        )
        to_north[8 + b] = passed
        to_south[8 + b] = passed


def arrange(dest, entries, packs, ground, edge_spill):
    outs = [(8, 8), (6, 8), (16, 8), (16, 8), (8,), (8,), (BLOCKS, 8), (BLOCKS, 8), (3 * BLOCKS, 8), (3 * BLOCKS, 8)]
    return pl.pallas_call(
        arrange_kernel,
        out_shape=[shape(*dims, SIDE) for dims in outs],
        in_specs=[SMEM] * 2 + [VMEM] * 9,
        out_specs=[VMEM] * len(outs),
        scratch_shapes=[pltpu.VMEM((BLOCKS, 8, SIDE), F32)] * 2,
        compiler_params=params(4),
        cost_estimate=cost(0, 0),
    )(dest, entries, *packs, *ground, edge_spill)


def along_edge(h, z, rough, flow, face_before, face_first, face_last):
    lane = lanes(8, SIDE)
    eta = h + z
    flux = face(
        eta, pltpu.roll(eta, SIDE - 1, 1), z, pltpu.roll(z, SIDE - 1, 1), rough,
        pltpu.roll(flow, 1, 1), flow, pltpu.roll(flow, SIDE - 1, 1),
    )
    flux = jnp.where(lane == 0, face_first, flux)
    flux = jnp.where(lane == SIDE - 1, face_last, flux)
    lower = jnp.where(lane == 0, face_before, pltpu.roll(flux, 1, 1))
    return lower - flux


def corner_faces(h, z, rough, flow, entry_s, entry_n, corners_s, corners_n):
    def chosen(entry, corners, q):
        value = jnp.zeros((8, SIDE), F32)
        for j in range(2 * BLOCKS):
            value = jnp.where(entry == j, corners[q][j : j + 1], value)
        return value

    h_s, t_s, z_s, n_s = (chosen(entry_s, corners_s, q) for q in range(4))
    h_n, t_n, z_n = (chosen(entry_n, corners_n, q) for q in range(3))
    last = SIDE - 1
    has_s = jnp.where(column(entry_s, 0) >= 0.0, 1.0, 0.0)
    has_n = jnp.where(column(entry_n, 0) >= 0.0, 1.0, 0.0)
    eta, eta_s, eta_n = h + z, h_s + z_s, h_n + z_n
    before = face(
        column(eta_s, last), column(eta, 0), column(z_s, last), column(z, 0), column(n_s, last),
        column(t_s, last - 1), column(t_s, last), column(flow, 0),
    ) * has_s
    first = face(
        column(eta, 0), column(eta, 1), column(z, 0), column(z, 1), column(rough, 0),
        column(t_s, last), column(flow, 0), column(flow, 1),
    )
    final = face(
        column(eta, last), column(eta_n, 0), column(z, last), column(z_n, 0), column(rough, last),
        column(flow, last - 1), column(flow, last), column(t_n, 0),
    ) * has_n
    return before, first, final


def edges_kernel(
    entries, wet, edge_spill, low, high, ground_low, ground_high, wide_low_in, wide_high_in, has_low_in, has_high_in,
    far_east, far_west, pack1, pack_back, to_south, to_north, from_north, from_south,
    columns, rows,
    wide_low, wide_high, has_low, has_high, wetness, edge, rim_low, rim_high, corners, stack,
):
    wide_low[...] = wide_low_in[...]
    wide_high[...] = wide_high_in[...]
    has_low[...] = has_low_in[...]
    has_high[...] = has_high_in[...]
    for b in range(BLOCKS):
        value = jnp.full((1, SIDE), wet[0, b].astype(F32), F32)
        wetness[b : b + 1] = value
        wetness[4 + b : 5 + b] = value
        for entry, near, far, wide, has in (
            (entries[0, b, 2], to_north, from_south, wide_low, has_low),
            (entries[0, b, 3], to_south, from_north, wide_high, has_high),
        ):
            put_rim(
                entry, 4 + b, lambda s, r=near: r[s], lambda s, r=near: r[BLOCKS + s],
                lambda s, r=far: r[s], lambda s, r=far: r[BLOCKS + s], wide, has,
            )
    for j in range(BLOCKS):
        near = slice(j, j + 1)
        far = slice(BLOCKS + j, BLOCKS + j + 1)
        for q, row in enumerate(
            (
                far_east[j, 1:2], far_east[j, 5:6], pack1[6 + j, 1:2], pack1[6 + j, 3:4],
                far_west[j, 0:1], far_west[j, 6:7], pack_back[1 + j, 0:1], pack_back[1 + j, 2:3],
            )
        ):
            for i, passed in enumerate((from_south, from_north)):
                corners[i, q, near] = row
                corners[i, q, far] = passed[2 * BLOCKS + j, q : q + 1]

    def seen(i, first):
        return [corners[i, first + q] for q in range(4)]

    h0, h1, h2, q0, q1, q2, t0, t1 = (low[q] for q in range(8))
    z0, z1, z2, n0, n1 = (ground_low[q] for q in range(5))
    hy, hz, qx, qy, qz, tz = (high[q] for q in range(6))
    zy, zz, ny, nz = (ground_high[q] for q in range(4))
    face_m, face_0, face_1 = faces_low(low, ground_low, wide_low)
    face_y, face_z = faces_high(high, ground_high, wide_high)
    face_m = face_m * has_low[...]
    face_z = face_z * has_high[...]
    swapped = [sides_swapped(f) for f in (face_m, face_0, face_z)]

    def beside(spot):
        return [column(f, spot) for f in swapped]

    wets = wetness[...]
    last = SIDE - 1
    new_0 = (h0 + RATIO * (face_m - face_0 + along_edge(h0, z0, n0, t0, *beside(0))) + edge_spill[0]) * wets
    new_1 = (h1 + RATIO * (face_0 - face_1 + along_edge(h1, z1, n1, t1, *beside(1))) + edge_spill[1]) * wets
    new_z = (hz + RATIO * (face_y - face_z + along_edge(hz, zz, nz, tz, *beside(last))) + edge_spill[2]) * wets
    flow_0, flow_1, flow_y, flow_z = (f * wets for f in (face_0, face_1, face_y, face_z))
    for i, value in enumerate((new_z, flow_y, flow_z, new_0, flow_0)):
        edge[i] = value

    sides = lax.broadcasted_iota(jnp.int32, (8, 1), 0) < 4
    ghy, ghz, gqx, gqy, gqz, gtz = (wide_low[q] for q in range(6))
    gzy, gzz, gny, gnz, gspill = (wide_low[8 + q] for q in range(5))
    across = corner_faces(ghz, gzz, gnz, gtz, wide_low[13], wide_low[14], seen(0, 0), seen(1, 0))
    given = [column(wide_low[13 + q], last) for q in range(3)]
    ends = [jnp.where(sides, a, g) for a, g in zip(across, given)]
    far_face = face(ghy + gzy, ghz + gzz, gzy, gzz, gny, gqx, gqy, gqz)
    far_low = (
        ghz + RATIO * (far_face - face_m + along_edge(ghz, gzz, gnz, gtz, *ends)) + gspill,
        far_face,
        face_m,
    )
    gh0, gh1, gq0, gq1, gt0 = (wide_high[q] for q in (0, 1, 3, 4, 6))
    gz0, gz1, gn0, gspill = (wide_high[8 + q] for q in range(4))
    across = corner_faces(gh0, gz0, gn0, gt0, wide_high[12], wide_high[13], seen(0, 4), seen(1, 4))
    given = [column(wide_high[12 + q], 0) for q in range(3)]
    ends = [jnp.where(sides, a, g) for a, g in zip(across, given)]
    far_face = face(gh0 + gz0, gh1 + gz1, gz0, gz1, gn0, qz, gq0, gq1)
    far_high = (
        gh0 + RATIO * (face_z - far_face + along_edge(gh0, gz0, gn0, gt0, *ends)) + gspill,
        far_face,
    )
    for rim, far_rows, first, group in ((rim_low, far_low, 0, 0), (rim_high, far_high, 3, 1)):
        for q, far_row in enumerate(far_rows):
            rim[q] = far_row
        for b in range(BLOCKS):
            for side in range(2):
                entry = entries[0, b, 2 * side + group]
                sub = slice(side * 4 + b, side * 4 + b + 1)
                near = pl.ds(side * 4 + jnp.clip(entry, 0, BLOCKS - 1), 1)
                for q in range(len(far_rows)):
                    row = jnp.where(entry >= BLOCKS, rim[q, sub], edge[first + q, near])
                    rim[q, sub] = jnp.where(entry >= 0, row, 0.0)

    hm, qmm, qm = (rim_low[q] for q in range(3))
    hp, qp = (rim_high[q] for q in range(2))
    zm, nm, zp = wide_low[9], wide_low[11], wide_high[8]
    next_m = face(hm + zm, new_0 + z0, zm, z0, nm, qmm, qm, flow_0) * has_low[...]
    next_0 = face(new_0 + z0, new_1 + z1, z0, z1, n0, qm, flow_0, flow_1)
    next_z = face(new_z + zz, hp + zp, zz, zp, nz, flow_y, flow_z, qp) * has_high[...]
    stack[...] = jnp.zeros_like(stack)
    rows[...] = jnp.zeros_like(rows)
    for b in range(BLOCKS):
        for i, value in enumerate((face_m, face_0, face_z, next_m, next_0, next_z)):
            stack[b * 8 + i : b * 8 + i + 1] = value[b : b + 1]
            rows[b, i : i + 1] = value[4 + b : 5 + b]
    turned = stack[...].T
    columns[0] = turned
    for b in range(1, BLOCKS):
        columns[b] = pltpu.roll(turned, HALF - 8 * b, 1)


def inflow_kernel(cells, rates, spill, edge_spill):
    spill[...] = jnp.zeros_like(spill)
    edge_spill[...] = jnp.zeros_like(edge_spill)
    lane = lanes(1, SIDE)
    for b in range(BLOCKS):

        def point(p, carry, b=b):
            cell = cells[0, b, p]
            row = lax.div(cell, SIDE)
            column = lax.rem(cell, SIDE)
            rate = GAIN * rates[0, b, p]
            at_column = jnp.where(lane == column, rate, 0.0)
            at_row = jnp.where(lane == row, rate, 0.0)
            line = pl.ds(row, 1)
            spill[b, line] = spill[b, line] + at_column
            for i, place in enumerate((0, 1, SIDE - 1)):
                edge_spill[i, b : b + 1] += jnp.where(column == place, at_row, 0.0)
                edge_spill[i, 4 + b : 5 + b] += jnp.where(row == place, at_column, 0.0)
            return carry

        lax.fori_loop(0, RIVERS, point, 0)


def lay_inflow(cells, rates):
    return pl.pallas_call(
        inflow_kernel,
        out_shape=[shape(BLOCKS, SIDE, SIDE), shape(3, 8, SIDE)],
        in_specs=[SMEM, SMEM],
        out_specs=[VMEM] * 2,
        compiler_params=params(4),
        cost_estimate=cost(0, 0),
    )(cells, rates)


def block_step(now, ground, spill, columns, rows, base, wetness, write):
    lane = lanes(ROWS, SIDE)
    sub = lax.broadcasted_iota(jnp.int32, (ROWS, SIDE), 0)

    def at(load, field, first, shift):
        if 0 <= first + shift <= SIDE - ROWS:
            return load(field, first + shift)
        return pltpu.roll(load(field, first), -shift % ROWS, 0)

    below = rows(base)
    for first in range(0, SIDE, ROWS):
        h, qx, qy = (at(now, f, first, 0) for f in range(3))
        z, rough = (at(ground, f, first, 0) for f in range(2))
        eta = h + z
        flux_x = face(
            eta, pltpu.roll(eta, SIDE - 1, 1), z, pltpu.roll(z, SIDE - 1, 1), rough,
            pltpu.roll(qx, 1, 1), qx, pltpu.roll(qx, SIDE - 1, 1),
        )
        edge = columns(pl.ds(first, ROWS))
        flux_x = jnp.where(lane == 0, edge[:, base + 1 : base + 2], flux_x)
        flux_x = jnp.where(lane == SIDE - 1, edge[:, base + 2 : base + 3], flux_x)
        flux_w = jnp.where(lane == 0, edge[:, base : base + 1], pltpu.roll(flux_x, 1, 1))
        z_up = at(ground, 0, first, 1)
        flux_y = face(
            eta, at(now, 0, first, 1) + z_up, z, z_up, rough, at(now, 2, first, -1), qy, at(now, 2, first, 1)
        )
        if first == 0:
            flux_y = jnp.where(sub == 0, rows(base + 1), flux_y)
        if first == SIDE - ROWS:
            flux_y = jnp.where(sub == ROWS - 1, rows(base + 2), flux_y)
        flux_s = jnp.where(sub == 0, below, pltpu.roll(flux_y, 1, 0))
        below = flux_y[ROWS - 1 : ROWS]
        depth = h + RATIO * (flux_w - flux_x + flux_s - flux_y) + spill(pl.ds(first, ROWS))
        write(first, depth * wetness, flux_x * wetness, flux_y * wetness)


def block(shifts, dest, wet, terrain, columns, rows, spill, states, out, then, done, sems):
    slot = landing_slot(dest, jnp.where(core() == 0, *shifts))
    wetness = wet[0, slot].astype(F32)
    state = states[0]
    if shifts == W_SHIFTS:
        for here, ref in enumerate(states):

            @pl.when(core() == 1 - here)
            def _(ref=ref):
                copy = pltpu.make_async_copy(ref, done, sems.at[0])
                copy.start()
                copy.wait()

        state = done
    copies = []

    def now(field, first):
        if shifts != A_SHIFTS:
            return state[field, first : first + ROWS]
        if first + ROWS <= CUT:
            return states[0][field, first : first + ROWS]
        if first >= CUT:
            return states[1][field, first - CUT : first - CUT + ROWS]
        return jnp.concatenate([states[0][field, first:CUT], states[1][field, 0 : first + ROWS - CUT]])

    def ground(field, first):
        return terrain[0, slot, field, first : first + ROWS]

    def keep(first, *fields):
        for f, value in enumerate(fields):
            then[f, first : first + ROWS] = value

    def finish(first, *fields):
        for f, value in enumerate(fields):
            done[f, first : first + ROWS] = value
        lines = pl.ds(first, ROWS)
        copies.append(pltpu.make_async_copy(done.at[:, lines], out.at[0, slot, :, lines], sems.at[len(copies)]))
        copies[-1].start()

    shared = (
        lambda at: spill[slot, at],
        lambda at: columns[slot, at],
        lambda q: rows[slot, q : q + 1],
    )
    block_step(now, ground, *shared, 0, wetness, keep)
    block_step(lambda f, first: then[f, first : first + ROWS], ground, *shared, 3, wetness, finish)
    return copies


EDGE_INPUTS = 19
EDGE_SCRATCH = 10


def block_scratch():
    return [pltpu.VMEM((3, SIDE, SIDE), F32)] * 3 + [pltpu.SemaphoreType.DMA((SIDE // ROWS,))] * 2


def early_kernel(dest, *refs):
    ins, refs = refs[:EDGE_INPUTS], refs[EDGE_INPUTS:]
    terrain, spill, own, a_low, a_high, out, columns, rows = refs[:8]
    edge_scratch, (then, done1, done2, sems1, sems2) = refs[8 : 8 + EDGE_SCRATCH], refs[8 + EDGE_SCRATCH :]
    edges_kernel(*ins, columns, rows, *edge_scratch)
    shared = (dest, ins[1], terrain, columns, rows, spill)
    copies = block(OWN_SHIFTS, *shared, (own,), out, then, done1, sems1)
    copies += block(A_SHIFTS, *shared, (a_low, a_high), out, then, done2, sems2)
    for copy in copies:
        copy.wait()


def early_blocks(dest, edge_inputs, terrain, spill, own, a_low, a_high):
    return pl.pallas_call(
        early_kernel,
        out_shape=[shape(1, BLOCKS, 3, SIDE, SIDE), shape(BLOCKS, SIDE, HALF), shape(BLOCKS, 8, SIDE)],
        in_specs=[SMEM] * 3 + [VMEM] * (EDGE_INPUTS - 2 + 5),
        out_specs=[HBM, VMEM, VMEM],
        scratch_shapes=[
            pltpu.VMEM((16, 8, SIDE), F32),
            pltpu.VMEM((16, 8, SIDE), F32),
            pltpu.VMEM((8, SIDE), F32),
            pltpu.VMEM((8, SIDE), F32),
            pltpu.VMEM((8, SIDE), F32),
            pltpu.VMEM((5, 8, SIDE), F32),
            pltpu.VMEM((3, 8, SIDE), F32),
            pltpu.VMEM((2, 8, SIDE), F32),
            pltpu.VMEM((2, 8, 8, SIDE), F32),
            pltpu.VMEM((HALF, SIDE), F32),
        ]
        + block_scratch(),
        compiler_params=params(16),
        cost_estimate=cost(0, 0),
    )(dest, *edge_inputs, terrain, spill, own, a_low, a_high)


def late_kernel(dest, wet, terrain, columns, rows, spill, arrived_w, relayed, arrived_x, _, out, *scratch):
    then, done1, done2, sems1, sems2 = scratch
    shared = (dest, wet, terrain, columns, rows, spill)
    copies = block(W_SHIFTS, *shared, (arrived_w, relayed), out, then, done1, sems1)
    copies += block(X_SHIFTS, *shared, (arrived_x,), out, then, done2, sems2)
    for copy in copies:
        copy.wait()


def late_blocks(dest, wet, terrain, columns, rows, spill, arrived_w, relayed, arrived_x, out):
    return pl.pallas_call(
        late_kernel,
        out_shape=shape(1, BLOCKS, 3, SIDE, SIDE),
        in_specs=[SMEM] * 2 + [VMEM] * 4 + [ANY] * 2 + [VMEM, HBM],
        out_specs=HBM,
        input_output_aliases={9: 0},
        scratch_shapes=block_scratch(),
        compiler_params=params(16),
        cost_estimate=cost(0, 0),
    )(dest, wet, terrain, columns, rows, spill, arrived_w, relayed, arrived_x, out)


def passed_along(x, axis, by, wrap=True):
    devices = lax.axis_size(axis)
    return lax.ppermute(x, axis, [(i, (i + by) % devices) for i in range(devices)])


def passed_to(x, target):
    devices = lax.axis_size("tile")
    pairs = [(i, target(i // 2, i % 2)) for i in range(devices)]
    return lax.ppermute(x, "tile", [(i, t % devices) for i, t in pairs if t is not None])


def back_one(chip):
    return chip // RING * RING + (chip - 1) % RING


def first_leg(chip, at):
    return 2 * chip + 1 if at == 0 else 2 * back_one(chip)


def second_leg(chip, at):
    sender = chip // RING * RING + (chip + 1) % RING
    return 2 * (sender + 2) if at == 0 else None


def next_chip_swapped(chip, at):
    return 2 * (chip + 1) + 1 - at


def body(flood_state, terrain, destination, wet_mask, neighbours, inflow_cells, inflow_rates):
    dest, state = in_hbm(destination), in_hbm(flood_state)
    a_low, a_high = pick_early(dest, state)
    arrived_low = passed_along(a_low, "tile", 2)
    own, block_w, block_x, ground_low, ground_high, *packs = prepare(
        dest, in_hbm(neighbours), state, a_low, a_high,
        in_hbm(terrain), in_hbm(inflow_cells), in_hbm(inflow_rates),
    )
    ground = (ground_low, ground_high)
    spill, edge_spill = lay_inflow(inflow_cells, inflow_rates)
    (packs[5],) = gate((packs[5],), (arrived_low,))
    packs = [packs[0]] + [passed_along(p, "tile", d) for d, p in zip((1, 2, 3, 4, -1), packs[1:])]
    a_high, block_x, block_w = gate((a_high, block_x, block_w), packs[1:])
    arrived_high = passed_along(a_high, "tile", 2)
    arrived_x = passed_to(block_x, next_chip_swapped)
    arrived_w = passed_to(block_w, first_leg)
    low, high, wide_low, wide_high, has_low, has_high, far_east, far_west, to_south, to_north = arrange(
        destination, neighbours, packs, ground, edge_spill
    )
    from_north = passed_along(to_south, "grp", -1)
    from_south = passed_along(to_north, "grp", 1)
    (arrived_w,) = gate((arrived_w,), (from_north, from_south, arrived_high))
    relayed = passed_to(arrived_w, second_leg)
    edge_inputs = (
        neighbours, wet_mask, edge_spill, low, high, *ground, wide_low, wide_high, has_low, has_high,
        far_east, far_west, packs[1], packs[5], to_south, to_north, from_north, from_south,
    )
    out, columns, rows = early_blocks(destination, edge_inputs, terrain, spill, own, arrived_low, arrived_high)
    return late_blocks(destination, wet_mask, terrain, columns, rows, spill, arrived_w, relayed, arrived_x, out)


def solution(mesh):
    in_specs = (
        P("grp", "tile", None, None, None),
        P("grp", "tile", None, None, None),
        P("grp", None),
        P("grp", "tile"),
        P("grp", "tile", None),
        P("grp", "tile", None),
        P("grp", "tile", None),
    )
    out_specs = P("grp", "tile", None, None, None)
    return jax.shard_map(body, mesh=mesh, in_specs=in_specs, out_specs=out_specs, check_vma=False)
```

profile of v0, /device:TPU:4, one launch (start us, length us, event | category | flops | bytes accessed | tf_op | source)
XLA Modules:
  0.0 64.3 jit_solution(14381756847900158837)
XLA Ops:
  0.0 1.9 %shard_map.74 = (f32[3,64,256]{2,1,0:T(8,128)S(1)}, f32[3,192,256]{2,1,0:T(8,128)S(1)}) custom-call(s32[1,128]{1,0:T(1,128)} %dest.9, f32[1,4,3,256,256]{4,3,2,1,0:T(8,128)} %state.3), custom_call_target="tpu_custom_call" | custom-call | tf_op jit(solution)/shard_map/pallas_call | solution.py:108
  1.9 2.0 %collective-permute-start.4 = (f32[3,64,256]{2,1,0:T(8,128)S(1)}, f32[3,64,256]{2,1,0:T(8,128)S(1)}, u32[]{:S(2)}, u32[]{:S(2)}) collective-permute-start(f32[3,64,256]{2,1,0:T(8,128)S(1)} %get-tuple-element.37.a_low), channel_id=1, source_target_pairs={{0,8},{4,12},{8,16},{12,20},{16,24},{20,28},{24,32},{28,36},{32,40... | collective-permute-start | bytes 589832 | tf_op jit(solution)/shard_map/ppermute | solution.py:706
  3.9 4.1 %shard_map.75 = (f32[3,256,256]{2,1,0:T(8,128)S(1)}, f32[3,256,256]{2,1,0:T(8,128)S(1)}, f32[3,256,256]{2,1,0:T(8,128)S(1)}, f32[5,8,256]{2,1,0:T(8,128)S(1)}, f...) custom-call(s32[1,128]{1,0:T(1,128)} %dest.9, ...), custom_call_target="tpu_custom_call" | custom-call | tf_op jit(solution)/shard_map/pallas_call | solution.py:215
  8.0 0.1 collective-permute-start
  8.1 2.0 %collective-permute-start.1 = (f32[6,8,256]{2,1,0:T(8,128)S(1)}, f32[6,8,256]{2,1,0:T(8,128)S(1)}, u32[]{:S(2)}, u32[]{:S(2)}) collective-permute-start(f32[6,8,256]{2,1,0:T(8,128)S(1)} %get-tuple-element.41), channel_id=1, source_target_pairs={{0,8},{4,12},{8,16},{12,20},{16,24},{20,28},{24,32},{28,36},{32,40... | collective-permute-start | bytes 147464 | tf_op jit(solution)/shard_map/ppermute | solution.py:706
  10.1 1.3 %collective-permute-start.2 = (f32[5,8,256]{2,1,0:T(8,128)S(1)}, f32[5,8,256]{2,1,0:T(8,128)S(1)}, u32[]{:S(2)}, u32[]{:S(2)}) collective-permute-start(f32[5,8,256]{2,1,0:T(8,128)S(1)} %get-tuple-element.42), channel_id=1, source_target_pairs={{0,12},{4,16},{8,20},{12,24},{16,28},{20,32},{24,36},{28,40},{32,4... | collective-permute-start | bytes 122888 | tf_op jit(solution)/shard_map/ppermute | solution.py:706
  11.4 2.0 %collective-permute-done.4.refs_1_.refs_22_ = f32[3,64,256]{2,1,0:T(8,128)S(1)} collective-permute-done((f32[3,64,256]{2,1,0:T(8,128)S(1)}, f32[3,64,256]{2,1,0:T(8,128)S(1)}, u32[]{:S(2)}, u32[]{:S(2)}) %collective-permute-start.4) | collective-permute-done | bytes 196640 | tf_op jit(solution)/shard_map/ppermute | solution.py:706
  13.3 2.9 %collective-permute-start.5 = (f32[5,8,256]{2,1,0:T(8,128)S(1)}, f32[5,8,256]{2,1,0:T(8,128)S(1)}, u32[]{:S(2)}, u32[]{:S(2)}) collective-permute-start(f32[5,8,256]{2,1,0:T(8,128)S(1)} %shard_map.76), channel_id=1, source_target_pairs={{0,124},{4,0},{8,4},{12,8},{16,12},{20,16},{24,20},{28,24},{32,28}... | collective-permute-start | bytes 122888 | tf_op jit(solution)/shard_map/ppermute | solution.py:706
  16.2 7.3 %collective-permute-done.3.pack4.refs_6_ = f32[1,8,256]{2,1,0:T(8,128)S(1)} collective-permute-done((f32[1,8,256]{2,1,0:T(8,128)S(1)}, f32[1,8,256]{2,1,0:T(8,128)S(1)}, u32[]{:S(2)}, u32[]{:S(2)}) %collective-permute-start.3) | collective-permute-done | bytes 8224 | tf_op jit(solution)/shard_map/ppermute | solution.py:706
  23.5 0.1 collective-permute-start.9
  23.6 0.1 collective-permute-start.8
  23.7 2.1 %shard_map.73 = (f32[4,256,256]{2,1,0:T(8,128)S(1)}, f32[3,8,256]{2,1,0:T(8,128)S(1)}) custom-call(s32[1,4,16]{2,1,0:T(4,128)S(1)} %copy-done.3, f32[1,4,16]{2,1,0:T(4,128)S(1)} %copy-done.4), custom_call_target="tpu_custom_call" | custom-call | tf_op jit(solution)/shard_map/pallas_call | solution.py:543
  25.8 1.1 %shard_map.77 = (f32[8,8,256]{2,1,0:T(8,128)S(1)}, f32[6,8,256]{2,1,0:T(8,128)S(1)}, f32[16,8,256]{2,1,0:T(8,128)S(1)}, f32[16,8,256]{2,1,0:T(8,128)S(1)}, f32[8...) custom-call(s32[1,128]{1,0:T(1,128)S(1)} %copy-done.2, ...), custom_call_target="tpu_custom_call" | custom-call | tf_op jit(solution)/shard_map/pallas_call | solution.py:355
  26.9 0.6 collective-permute-start.6
  27.5 1.5 %collective-permute-start.7 = (f32[12,8,256]{2,1,0:T(8,128)S(1)}, f32[12,8,256]{2,1,0:T(8,128)S(1)}, u32[]{:S(2)}, u32[]{:S(2)}) collective-permute-start(f32[12,8,256]{2,1,0:T(8,128)S(1)} %get-tuple-element.56.refs_16_), channel_id=1, source_target_pairs={{0,1},{1,2},{2,3},{3,0},{4,5},{5,6},{6,7},{7,4},{8,9},{9,10},{10,1... | collective-permute-start | bytes 294920 | tf_op jit(solution)/shard_map/ppermute | solution.py:706
  29.0 1.1 %collective-permute-start.11 = (f32[3,256,256]{2,1,0:T(8,128)S(1)}, f32[3,256,256]{2,1,0:T(8,128)S(1)}, u32[]{:S(2)}, u32[]{:S(2)}) collective-permute-start(f32[3,256,256]{2,1,0:T(8,128)S(1)} %get-tuple-element.65), channel_id=1, source_target_pairs={{0,12},{4,8},{8,20},{12,16},{16,28},{20,24},{24,36},{28,32},{32,44... | collective-permute-start | bytes 2359304 | tf_op jit(solution)/shard_map/ppermute | solution.py:712
  30.1 1.8 %collective-permute-done.6.refs_17_.refs_1_ = f32[12,8,256]{2,1,0:T(8,128)S(1)} collective-permute-done((f32[12,8,256]{2,1,0:T(8,128)S(1)}, f32[12,8,256]{2,1,0:T(8,128)S(1)}, u32[]{:S(2)}, u32[]{:S(2)}) %collective-permute-start.6) | collective-permute-done | bytes 98336 | tf_op jit(solution)/shard_map/ppermute | solution.py:706
  31.9 0.9 %collective-permute-done.7.refs_18_.refs_2_ = f32[12,8,256]{2,1,0:T(8,128)S(1)} collective-permute-done((f32[12,8,256]{2,1,0:T(8,128)S(1)}, f32[12,8,256]{2,1,0:T(8,128)S(1)}, u32[]{:S(2)}, u32[]{:S(2)}) %collective-permute-start.7) | collective-permute-done | bytes 98336 | tf_op jit(solution)/shard_map/ppermute | solution.py:706
  32.8 10.3 %collective-permute-done.8.refs_23_.refs_3_ = f32[3,192,256]{2,1,0:T(8,128)S(1)} collective-permute-done((f32[3,192,256]{2,1,0:T(8,128)S(1)}, f32[3,192,256]{2,1,0:T(8,128)S(1)}, u32[]{:S(2)}, u32[]{:S(2)}) %collective-permute-start.8) | collective-permute-done | bytes 589856 | tf_op jit(solution)/shard_map/ppermute | solution.py:706
  43.1 1.9 %collective-permute-start.10 = (f32[3,256,256]{2,1,0:T(8,128)S(1)}, f32[3,256,256]{2,1,0:T(8,128)S(1)}, u32[]{:S(2)}, u32[]{:S(2)}) collective-permute-start(f32[3,256,256]{2,1,0:T(8,128)S(1)} %shard_map.80.arrived_w), channel_id=1, source_target_pairs={{0,24},{8,32},{16,40},{24,16},{32,56},{40,64},{48,72},{56,48},{64,... | collective-permute-start | bytes 2359304 | tf_op jit(solution)/shard_map/ppermute | solution.py:712
  45.0 5.4 %shard_map.79 = (f32[1,4,3,256,256]{4,3,2,1,0:T(8,128)}, f32[4,256,128]{2,1,0:T(8,128)S(1)}, f32[4,8,256]{2,1,0:T(8,128)S(1)}) custom-call(s32[1,128]{1,0:T(1,128)S(1)} %copy-done.2, s32[1,4,4]{2,1,0:T(4,128)S(1)} %copy-done.1, s32[1,4]{1,0:T(1,128)S(1)} %copy-done.5, f32[3,8,256]{2,1,0:T(8,128)S(1)} %get-tuple-element.36.edge_spill.refs_2_, ...), custom_call_target="tpu_custom_call" | custom-call | tf_op jit(solution)/shard_map/pallas_call | solution.py:659
  50.4 2.7 %collective-permute-done.11.arrived_x = f32[3,256,256]{2,1,0:T(8,128)S(1)} collective-permute-done((f32[3,256,256]{2,1,0:T(8,128)S(1)}, f32[3,256,256]{2,1,0:T(8,128)S(1)}, u32[]{:S(2)}, u32[]{:S(2)}) %collective-permute-start.11) | collective-permute-done | bytes 786464 | tf_op jit(solution)/shard_map/ppermute | solution.py:712
  53.1 5.9 %collective-permute-done.10.relayed = f32[3,256,256]{2,1,0:T(8,128)S(1)} collective-permute-done((f32[3,256,256]{2,1,0:T(8,128)S(1)}, f32[3,256,256]{2,1,0:T(8,128)S(1)}, u32[]{:S(2)}, u32[]{:S(2)}) %collective-permute-start.10) | collective-permute-done | bytes 786464 | tf_op jit(solution)/shard_map/ppermute | solution.py:712
  59.1 5.0 %shard_map.81 = f32[1,4,3,256,256]{4,3,2,1,0:T(8,128)} custom-call(s32[1,128]{1,0:T(1,128)S(1)} %copy-done.2, s32[1,4]{1,0:T(1,128)S(1)} %copy-done.5, f32[1,4,2,256,256]{4,3,2,1,0:T(8,128)S(1)} %copy-done, f32[4,256,128]{2,1,0:T(8,128)S(1)} %get-tuple-element.62.columns, f32[4,8,256]{2,1,0:T(8,128)S(1)} %get-tuple-element.63.rows, ...), custom_call_target="tpu_custom_call", output_to_operand_aliasing={{}: (9, {})} | custom-call | tf_op jit(solution)/shard_map/pallas_call | solution.py:692
  (21 shorter events, 0.0 us)
Async XLA Ops:
  1.9 11.5 %collective-permute-start.4 = (f32[3,64,256]{2,1,0:T(8,128)S(1)}, f32[3,64,256]{2,1,0:T(8,128)S(1)}, u32[]{:S(2)}, u32[]{:S(2)}) collective-permute-start(f32[3,64,256]{2,1,0:T(8,128)S(1)} %get-tuple-element.37.a_low), channel_id=1, source_target_pairs={{0,8},{4,12},{8,16},{12,20},{16,24},{20,28},{24,32},{28,36},{32,40... | collective-permute-start | bytes 589832 | tf_op jit(solution)/shard_map/ppermute | solution.py:706
  3.9 19.8 %copy-start.3 = (s32[1,4,16]{2,1,0:T(4,128)S(1)}, s32[1,4,16]{2,1,0:T(4,128)}, u32[]{:S(2)}) copy-start(s32[1,4,16]{2,1,0:T(4,128)} %cells.3) | copy-start | bytes 772
  3.9 19.8 %copy-start.4 = (f32[1,4,16]{2,1,0:T(4,128)S(1)}, f32[1,4,16]{2,1,0:T(4,128)}, u32[]{:S(2)}) copy-start(f32[1,4,16]{2,1,0:T(4,128)} %rates.3) | copy-start | bytes 772
  3.9 21.9 %copy-start.1 = (s32[1,4,4]{2,1,0:T(4,128)S(1)}, s32[1,4,4]{2,1,0:T(4,128)}, u32[]{:S(2)}) copy-start(s32[1,4,4]{2,1,0:T(4,128)} %refs_0_.1) | copy-start | bytes 196
  3.9 21.9 %copy-start.2 = (s32[1,128]{1,0:T(1,128)S(1)}, s32[1,128]{1,0:T(1,128)}, u32[]{:S(2)}) copy-start(s32[1,128]{1,0:T(1,128)} %dest.9) | copy-start | bytes 1540
  8.0 37.0 %copy-start = (f32[1,4,2,256,256]{4,3,2,1,0:T(8,128)S(1)}, f32[1,4,2,256,256]{4,3,2,1,0:T(8,128)}, u32[]{:S(2)}) copy-start(f32[1,4,2,256,256]{4,3,2,1,0:T(8,128)} %terrain.1) | copy-start | bytes 6291460
  8.0 37.0 %copy-start.5 = (s32[1,4]{1,0:T(1,128)S(1)}, s32[1,4]{1,0:T(1,128)}, u32[]{:S(2)}) copy-start(s32[1,4]{1,0:T(1,128)} %wet.1) | copy-start | bytes 52
  8.0 15.5 %collective-permute-start = (f32[10,8,256]{2,1,0:T(8,128)S(1)}, f32[10,8,256]{2,1,0:T(8,128)S(1)}, u32[]{:S(2)}, u32[]{:S(2)}) collective-permute-start(f32[10,8,256]{2,1,0:T(8,128)S(1)} %get-tuple-element.40), channel_id=1, source_target_pairs={{0,4},{4,8},{8,12},{12,16},{16,20},{20,24},{24,28},{28,32},{32,36}... | collective-permute-start | bytes 245768 | tf_op jit(solution)/shard_map/ppermute | solution.py:706
  8.1 15.4 %collective-permute-start.1 = (f32[6,8,256]{2,1,0:T(8,128)S(1)}, f32[6,8,256]{2,1,0:T(8,128)S(1)}, u32[]{:S(2)}, u32[]{:S(2)}) collective-permute-start(f32[6,8,256]{2,1,0:T(8,128)S(1)} %get-tuple-element.41), channel_id=1, source_target_pairs={{0,8},{4,12},{8,16},{12,20},{16,24},{20,28},{24,32},{28,36},{32,40... | collective-permute-start | bytes 147464 | tf_op jit(solution)/shard_map/ppermute | solution.py:706
  10.1 13.4 %collective-permute-start.2 = (f32[5,8,256]{2,1,0:T(8,128)S(1)}, f32[5,8,256]{2,1,0:T(8,128)S(1)}, u32[]{:S(2)}, u32[]{:S(2)}) collective-permute-start(f32[5,8,256]{2,1,0:T(8,128)S(1)} %get-tuple-element.42), channel_id=1, source_target_pairs={{0,12},{4,16},{8,20},{12,24},{16,28},{20,32},{24,36},{28,40},{32,4... | collective-permute-start | bytes 122888 | tf_op jit(solution)/shard_map/ppermute | solution.py:706
  13.3 10.1 %collective-permute-start.5 = (f32[5,8,256]{2,1,0:T(8,128)S(1)}, f32[5,8,256]{2,1,0:T(8,128)S(1)}, u32[]{:S(2)}, u32[]{:S(2)}) collective-permute-start(f32[5,8,256]{2,1,0:T(8,128)S(1)} %shard_map.76), channel_id=1, source_target_pairs={{0,124},{4,0},{8,4},{12,8},{16,12},{20,16},{24,20},{28,24},{32,28}... | collective-permute-start | bytes 122888 | tf_op jit(solution)/shard_map/ppermute | solution.py:706
  16.2 7.3 %collective-permute-start.3 = (f32[1,8,256]{2,1,0:T(8,128)S(1)}, f32[1,8,256]{2,1,0:T(8,128)S(1)}, u32[]{:S(2)}, u32[]{:S(2)}) collective-permute-start(f32[1,8,256]{2,1,0:T(8,128)S(1)} %get-tuple-element.43), channel_id=1, source_target_pairs={{0,16},{4,20},{8,24},{12,28},{16,32},{20,36},{24,40},{28,44},{32,4... | collective-permute-start | bytes 24584 | tf_op jit(solution)/shard_map/ppermute | solution.py:706
  23.5 19.6 %collective-permute-start.9 = (f32[3,256,256]{2,1,0:T(8,128)S(1)}, f32[3,256,256]{2,1,0:T(8,128)S(1)}, u32[]{:S(2)}, u32[]{:S(2)}) collective-permute-start(f32[3,256,256]{2,1,0:T(8,128)S(1)} %get-tuple-element.64), channel_id=1, source_target_pairs={{0,4},{4,24},{8,12},{12,0},{16,20},{20,8},{24,28},{28,16},{32,36},... | collective-permute-start | bytes 2359304 | tf_op jit(solution)/shard_map/ppermute | solution.py:712
  23.6 19.5 %collective-permute-start.8 = (f32[3,192,256]{2,1,0:T(8,128)S(1)}, f32[3,192,256]{2,1,0:T(8,128)S(1)}, u32[]{:S(2)}, u32[]{:S(2)}) collective-permute-start(f32[3,192,256]{2,1,0:T(8,128)S(1)} %get-tuple-element.61), channel_id=1, source_target_pairs={{0,8},{4,12},{8,16},{12,20},{16,24},{20,28},{24,32},{28,36},{32,40... | collective-permute-start | bytes 1769480 | tf_op jit(solution)/shard_map/ppermute | solution.py:706
  26.9 5.0 %collective-permute-start.6 = (f32[12,8,256]{2,1,0:T(8,128)S(1)}, f32[12,8,256]{2,1,0:T(8,128)S(1)}, u32[]{:S(2)}, u32[]{:S(2)}) collective-permute-start(f32[12,8,256]{2,1,0:T(8,128)S(1)} %get-tuple-element.55.refs_15_), channel_id=1, source_target_pairs={{0,3},{1,0},{2,1},{3,2},{4,7},{5,4},{6,5},{7,6},{8,11},{9,8},{10,9... | collective-permute-start | bytes 294920 | tf_op jit(solution)/shard_map/ppermute | solution.py:706
  27.5 5.2 %collective-permute-start.7 = (f32[12,8,256]{2,1,0:T(8,128)S(1)}, f32[12,8,256]{2,1,0:T(8,128)S(1)}, u32[]{:S(2)}, u32[]{:S(2)}) collective-permute-start(f32[12,8,256]{2,1,0:T(8,128)S(1)} %get-tuple-element.56.refs_16_), channel_id=1, source_target_pairs={{0,1},{1,2},{2,3},{3,0},{4,5},{5,6},{6,7},{7,4},{8,9},{9,10},{10,1... | collective-permute-start | bytes 294920 | tf_op jit(solution)/shard_map/ppermute | solution.py:706
  29.0 24.1 %collective-permute-start.11 = (f32[3,256,256]{2,1,0:T(8,128)S(1)}, f32[3,256,256]{2,1,0:T(8,128)S(1)}, u32[]{:S(2)}, u32[]{:S(2)}) collective-permute-start(f32[3,256,256]{2,1,0:T(8,128)S(1)} %get-tuple-element.65), channel_id=1, source_target_pairs={{0,12},{4,8},{8,20},{12,16},{16,28},{20,24},{24,36},{28,32},{32,44... | collective-permute-start | bytes 2359304 | tf_op jit(solution)/shard_map/ppermute | solution.py:712
  43.1 16.0 %collective-permute-start.10 = (f32[3,256,256]{2,1,0:T(8,128)S(1)}, f32[3,256,256]{2,1,0:T(8,128)S(1)}, u32[]{:S(2)}, u32[]{:S(2)}) collective-permute-start(f32[3,256,256]{2,1,0:T(8,128)S(1)} %shard_map.80.arrived_w), channel_id=1, source_target_pairs={{0,24},{8,32},{16,40},{24,16},{32,56},{40,64},{48,72},{56,48},{64,... | collective-permute-start | bytes 2359304 | tf_op jit(solution)/shard_map/ppermute | solution.py:712
where the time goes:
time: 64.5 us; the launch traced here: 64.3 us
  waiting for transfers between devices  30.9 us (48%)
  Pallas kernels  19.6 us (30%)
  starting transfers between devices  13.4 us (21%)
    ppermute x9, waiting for transfers between devices, passed_along(): lax.ppermute(x, axis, [(i, (i + by) % devices) for i in range(devices)])  22.2 us
    ppermute x9, starting transfers between devices, passed_along(): lax.ppermute(x, axis, [(i, (i + by) % devices) for i in range(devices)])  10.4 us
    ppermute x3, waiting for transfers between devices, passed_to(): lax.ppermute(x, 'tile', [(i, t % devices) for i, t in pairs if t is not N...  8.65 us
    pallas_call x1, Pallas kernels, early_blocks(): pl.pallas_call(early_kernel, out_shape=[shape(1, BLOCKS, 3, SIDE, SIDE),...  5.39 us
    pallas_call x1, Pallas kernels, late_blocks(): pl.pallas_call(late_kernel, out_shape=shape(1, BLOCKS, 3, SIDE, SIDE), in...  5.04 us
    pallas_call x1, Pallas kernels, prepare(): pl.pallas_call(prepare_kernel, out_shape=[shape(3, SIDE, SIDE)] * 3 + [sh...  4.09 us
    ppermute x3, starting transfers between devices, passed_to(): lax.ppermute(x, 'tile', [(i, t % devices) for i, t in pairs if t is not N...  3.07 us
    pallas_call x1, Pallas kernels, lay_inflow(): pl.pallas_call(inflow_kernel, out_shape=[shape(BLOCKS, SIDE, SIDE), shape...  2.11 us
  transfers between devices with their start and end apart: 12, of which 7 were waited for; matrix products, arithmetic and copies ran while one was open for 0% of the time, Pallas kernels for 20%

commit v1 on v0

--- a/solution.py
+++ b/solution.py
@@ -26,7 +26,6 @@
 SMEM = pl.BlockSpec(memory_space=pltpu.SMEM)
 HBM = pl.BlockSpec(memory_space=pltpu.HBM)
 RING = 4
-CUT = 64
 OWN_SHIFTS = (0, 0)
 A_SHIFTS = (2, 2)
 W_SHIFTS = (3, 1)
@@ -91,13 +90,13 @@
     return pltpu.with_memory_space_constraint(x, pltpu.HBM)
 
 
-def pick_kernel(dest, state, a_low, a_high, sems):
-    slot = leaving_slot(dest, 2)
-    parts = (
-        (state.at[0, slot, :, pl.ds(0, CUT)], a_low),
-        (state.at[0, slot, :, pl.ds(CUT, SIDE - CUT)], a_high),
-    )
-    loads = [pltpu.make_async_copy(part, ref, sems.at[i]) for i, (part, ref) in enumerate(parts)]
+def pick_kernel(dest, state, block_a, block_w, sems):
+    slots = [leaving_slot(dest, k) for k in range(1, BLOCKS)]
+    slot_w = jnp.where(core() == 0, slots[0], slots[2])
+    loads = [
+        pltpu.make_async_copy(state.at[0, slot], ref, sems.at[i])
+        for i, (slot, ref) in enumerate(((slots[1], block_a), (slot_w, block_w)))
+    ]
     for load in loads:
         load.start()
     for load in loads:
@@ -107,7 +106,7 @@
 def pick_early(dest, state):
     return pl.pallas_call(
         pick_kernel,
-        out_shape=[shape(3, CUT, SIDE), shape(3, SIDE - CUT, SIDE)],
+        out_shape=[shape(3, SIDE, SIDE)] * 2,
         in_specs=[SMEM, HBM],
         out_specs=[VMEM] * 2,
         scratch_shapes=[pltpu.SemaphoreType.DMA((2,))],
@@ -117,30 +116,23 @@
 
 
 def prepare_kernel(
-    dest, entries, state, a_low, a_high, ground_in, cells, rates,
-    own, block_w, block_x, low, high, pack0, pack1, pack2, pack3, pack4, pack_back, terrain, sems,
+    dest, entries, state, block_a, block_w, ground_in, cells, rates,
+    own, block_x, low, high, pack0, pack1, pack2, pack3, pack4, pack_back, terrain, sems,
 ):
     slots = [leaving_slot(dest, k) for k in range(BLOCKS)]
     first_core = core() == 0
-    slot_w = jnp.where(first_core, slots[1], slots[3])
     slot_x = jnp.where(first_core, slots[3], slots[1])
-    held = (block_w, block_x, own)
+    held = (block_x, own)
     loads = [pltpu.make_async_copy(ground_in, terrain, sems.at[3])]
-    for i, (slot, ref) in enumerate(zip((slot_w, slot_x, slots[0]), held)):
+    for i, (slot, ref) in enumerate(zip((slot_x, slots[0]), held)):
         loads.append(pltpu.make_async_copy(state.at[0, slot], ref, sems.at[i]))
     for load in loads:
         load.start()
     lane = lanes(SIDE, HALF)
 
-    def strips(parts, write):
-        ref, tail = parts[0], parts[-1]
-        size = tail.shape[1]
-
-        def half(columns):
-            return [jnp.concatenate([part[f, :, columns] for part in parts]) for f in range(3)]
-
-        west = half(slice(0, HALF))
-        east = half(slice(HALF, SIDE))
+    def strips(ref, write):
+        west = [ref[f, :, :HALF] for f in range(3)]
+        east = [ref[f, :, HALF:] for f in range(3)]
         packed = jnp.where(lane < 3, west[0], pltpu.roll(west[1], 3, 1))
         packed = jnp.where(lane < 6, packed, pltpu.roll(west[2], 6, 1))
         packed = jnp.where(lane < 8, packed, pltpu.roll(east[0], 10, 1))
@@ -149,7 +141,7 @@
         turned = packed.T
         south = jnp.concatenate([ref[0, 0:3], ref[2, 0:3], ref[1, 0:2]])
         north = jnp.concatenate(
-            [tail[0, size - 2 : size], tail[2, size - 3 : size], tail[1, size - 1 : size], jnp.zeros((2, SIDE), F32)]
+            [ref[0, SIDE - 2 : SIDE], ref[2, SIDE - 3 : SIDE], ref[1, SIDE - 1 : SIDE], jnp.zeros((2, SIDE), F32)]
         )
         write(turned[0:8], south, turned[8:16], north)
 
@@ -170,7 +162,8 @@
 
         return both
 
-    strips((a_low, a_high), functools.partial(write, 2))
+    strips(block_a, functools.partial(write, 2))
+    strips(block_w, write_by_core(1, 3))
     along = lanes(BLOCKS, SIDE)
     spills = [jnp.zeros((BLOCKS, SIDE), F32) for _ in range(2)]
     for p in range(RIVERS):
@@ -204,26 +197,26 @@
         pack_back[1 + b] = jnp.concatenate(
             [low[0, line], low[1, line], low[3, line], spills[0][line]] + links + blank * 2
         )
-    writers = (write_by_core(1, 3), write_by_core(3, 1), functools.partial(write, 0))
+    writers = (write_by_core(3, 1), functools.partial(write, 0))
     for load, ref, write_out in zip(loads[1:], held, writers):
         load.wait()
-        strips((ref,), write_out)
-
-
-def prepare(dest, entries, state, a_low, a_high, terrain, cells, rates):
+        strips(ref, write_out)
+
+
+def prepare(dest, entries, state, block_a, block_w, terrain, cells, rates):
     packs = [shape(count, 8, SIDE) for count in (5, 10, 6, 5, 1, 5)]
     return pl.pallas_call(
         prepare_kernel,
-        out_shape=[shape(3, SIDE, SIDE)] * 3 + [shape(5, 8, SIDE), shape(4, 8, SIDE)] + packs,
+        out_shape=[shape(3, SIDE, SIDE)] * 2 + [shape(5, 8, SIDE), shape(4, 8, SIDE)] + packs,
         in_specs=[SMEM, SMEM, HBM, VMEM, VMEM, HBM, VMEM, VMEM],
-        out_specs=[VMEM] * 11,
+        out_specs=[VMEM] * 10,
         scratch_shapes=[
             pltpu.VMEM((1, BLOCKS, 2, SIDE, SIDE), F32),
             pltpu.SemaphoreType.DMA((BLOCKS,)),
         ],
         compiler_params=params(12),
         cost_estimate=cost(0, 0),
-    )(dest, entries, state, a_low, a_high, terrain, cells, rates)
+    )(dest, entries, state, block_a, block_w, terrain, cells, rates)
 
 
 def gate_kernel(count, *refs):
@@ -603,13 +596,7 @@
     copies = []
 
     def now(field, first):
-        if shifts != A_SHIFTS:
-            return state[field, first : first + ROWS]
-        if first + ROWS <= CUT:
-            return states[0][field, first : first + ROWS]
-        if first >= CUT:
-            return states[1][field, first - CUT : first - CUT + ROWS]
-        return jnp.concatenate([states[0][field, first:CUT], states[1][field, 0 : first + ROWS - CUT]])
+        return state[field, first : first + ROWS]
 
     def ground(field, first):
         return terrain[0, slot, field, first : first + ROWS]
@@ -645,21 +632,24 @@
 
 def early_kernel(dest, *refs):
     ins, refs = refs[:EDGE_INPUTS], refs[EDGE_INPUTS:]
-    terrain, spill, own, a_low, a_high, out, columns, rows = refs[:8]
-    edge_scratch, (then, done1, done2, sems1, sems2) = refs[8 : 8 + EDGE_SCRATCH], refs[8 + EDGE_SCRATCH :]
+    terrain, spill, own, arrived_a, arrived_w, relayed, out, columns, rows = refs[:9]
+    edge_scratch, (then, done1, done2, sems1, sems2) = refs[9 : 9 + EDGE_SCRATCH], refs[9 + EDGE_SCRATCH :]
     edges_kernel(*ins, columns, rows, *edge_scratch)
     shared = (dest, ins[1], terrain, columns, rows, spill)
     copies = block(OWN_SHIFTS, *shared, (own,), out, then, done1, sems1)
-    copies += block(A_SHIFTS, *shared, (a_low, a_high), out, then, done2, sems2)
+    later = block(A_SHIFTS, *shared, (arrived_a,), out, then, done2, sems2)
     for copy in copies:
         copy.wait()
-
-
-def early_blocks(dest, edge_inputs, terrain, spill, own, a_low, a_high):
+    later += block(W_SHIFTS, *shared, (arrived_w, relayed), out, then, done1, sems1)
+    for copy in later:
+        copy.wait()
+
+
+def early_blocks(dest, edge_inputs, terrain, spill, own, arrived_a, arrived_w, relayed):
     return pl.pallas_call(
         early_kernel,
         out_shape=[shape(1, BLOCKS, 3, SIDE, SIDE), shape(BLOCKS, SIDE, HALF), shape(BLOCKS, 8, SIDE)],
-        in_specs=[SMEM] * 3 + [VMEM] * (EDGE_INPUTS - 2 + 5),
+        in_specs=[SMEM] * 3 + [VMEM] * (EDGE_INPUTS - 2 + 4) + [ANY] * 2,
         out_specs=[HBM, VMEM, VMEM],
         scratch_shapes=[
             pltpu.VMEM((16, 8, SIDE), F32),
@@ -676,29 +666,26 @@
         + block_scratch(),
         compiler_params=params(16),
         cost_estimate=cost(0, 0),
-    )(dest, *edge_inputs, terrain, spill, own, a_low, a_high)
-
-
-def late_kernel(dest, wet, terrain, columns, rows, spill, arrived_w, relayed, arrived_x, _, out, *scratch):
-    then, done1, done2, sems1, sems2 = scratch
+    )(dest, *edge_inputs, terrain, spill, own, arrived_a, arrived_w, relayed)
+
+
+def late_kernel(dest, wet, terrain, columns, rows, spill, arrived_x, _, out, then, done, sems):
     shared = (dest, wet, terrain, columns, rows, spill)
-    copies = block(W_SHIFTS, *shared, (arrived_w, relayed), out, then, done1, sems1)
-    copies += block(X_SHIFTS, *shared, (arrived_x,), out, then, done2, sems2)
-    for copy in copies:
+    for copy in block(X_SHIFTS, *shared, (arrived_x,), out, then, done, sems):
         copy.wait()
 
 
-def late_blocks(dest, wet, terrain, columns, rows, spill, arrived_w, relayed, arrived_x, out):
+def late_blocks(dest, wet, terrain, columns, rows, spill, arrived_x, out):
     return pl.pallas_call(
         late_kernel,
         out_shape=shape(1, BLOCKS, 3, SIDE, SIDE),
-        in_specs=[SMEM] * 2 + [VMEM] * 4 + [ANY] * 2 + [VMEM, HBM],
+        in_specs=[SMEM] * 2 + [VMEM] * 5 + [HBM],
         out_specs=HBM,
-        input_output_aliases={9: 0},
-        scratch_shapes=block_scratch(),
+        input_output_aliases={7: 0},
+        scratch_shapes=[pltpu.VMEM((3, SIDE, SIDE), F32)] * 2 + [pltpu.SemaphoreType.DMA((SIDE // ROWS,))],
         compiler_params=params(16),
         cost_estimate=cost(0, 0),
-    )(dest, wet, terrain, columns, rows, spill, arrived_w, relayed, arrived_x, out)
+    )(dest, wet, terrain, columns, rows, spill, arrived_x, out)
 
 
 def passed_along(x, axis, by, wrap=True):
@@ -731,33 +718,35 @@
 
 def body(flood_state, terrain, destination, wet_mask, neighbours, inflow_cells, inflow_rates):
     dest, state = in_hbm(destination), in_hbm(flood_state)
-    a_low, a_high = pick_early(dest, state)
-    arrived_low = passed_along(a_low, "tile", 2)
-    own, block_w, block_x, ground_low, ground_high, *packs = prepare(
-        dest, in_hbm(neighbours), state, a_low, a_high,
+    block_a, block_w = pick_early(dest, state)
+    arrived_a = passed_along(block_a, "tile", 2)
+    arrived_w = passed_to(block_w, first_leg)
+    own, block_x, ground_low, ground_high, *packs = prepare(
+        dest, in_hbm(neighbours), state, block_a, block_w,
         in_hbm(terrain), in_hbm(inflow_cells), in_hbm(inflow_rates),
     )
     ground = (ground_low, ground_high)
     spill, edge_spill = lay_inflow(inflow_cells, inflow_rates)
-    (packs[5],) = gate((packs[5],), (arrived_low,))
-    packs = [packs[0]] + [passed_along(p, "tile", d) for d, p in zip((1, 2, 3, 4, -1), packs[1:])]
-    a_high, block_x, block_w = gate((a_high, block_x, block_w), packs[1:])
-    arrived_high = passed_along(a_high, "tile", 2)
+    packs[5] = passed_along(packs[5], "tile", -1)
+    packs[1:3] = [passed_along(packs[d], "tile", d) for d in (1, 2)]
+    packs[3], packs[4], arrived_w = gate((packs[3], packs[4], arrived_w), (packs[5], edge_spill))
+    packs[3:5] = [passed_along(packs[d], "tile", d) for d in (3, 4)]
+    block_x, arrived_w = gate((block_x, arrived_w), (*packs[1:5], arrived_a))
     arrived_x = passed_to(block_x, next_chip_swapped)
-    arrived_w = passed_to(block_w, first_leg)
+    relayed = passed_to(arrived_w, second_leg)
     low, high, wide_low, wide_high, has_low, has_high, far_east, far_west, to_south, to_north = arrange(
         destination, neighbours, packs, ground, edge_spill
     )
     from_north = passed_along(to_south, "grp", -1)
     from_south = passed_along(to_north, "grp", 1)
-    (arrived_w,) = gate((arrived_w,), (from_north, from_south, arrived_high))
-    relayed = passed_to(arrived_w, second_leg)
     edge_inputs = (
         neighbours, wet_mask, edge_spill, low, high, *ground, wide_low, wide_high, has_low, has_high,
         far_east, far_west, packs[1], packs[5], to_south, to_north, from_north, from_south,
     )
-    out, columns, rows = early_blocks(destination, edge_inputs, terrain, spill, own, arrived_low, arrived_high)
-    return late_blocks(destination, wet_mask, terrain, columns, rows, spill, arrived_w, relayed, arrived_x, out)
+    out, columns, rows = early_blocks(
+        destination, edge_inputs, terrain, spill, own, arrived_a, arrived_w, relayed
+    )
+    return late_blocks(destination, wet_mask, terrain, columns, rows, spill, arrived_x, out)
 
 
 def solution(mesh):

time: 64.5 us -> 58 us (0.90)
  waiting for transfers between devices: 30.9 us -> 19.7 us
  starting transfers between devices: 13.4 us -> 17.5 us
    ppermute x9 -> x8, waiting for transfers between devices: 22.2 us -> 12.3 us  [passed_along(): lax.ppermute(x, axis, [(i, (i + by) % devices) for i in range(devices)])]
    ppermute x9 -> x8, starting transfers between devices: 10.4 us -> 15.2 us  [passed_along(): lax.ppermute(x, axis, [(i, (i + by) % devices) for i in range(devices)])]
    pallas_call x1, Pallas kernels: 5.39 us -> 7.73 us  [early_blocks(): pl.pallas_call(early_kernel, out_shape=[shape(1, BLOCKS, 3, SIDE, SIDE),...]
    pallas_call x1, Pallas kernels: 5.04 us -> 3 us  [late_blocks(): pl.pallas_call(late_kernel, out_shape=shape(1, BLOCKS, 3, SIDE, SIDE), in...]
    ppermute x3, waiting for transfers between devices: 8.65 us -> 7.4 us  [passed_to(): lax.ppermute(x, 'tile', [(i, t % devices) for i, t in pairs if t is not N...]
    ppermute x3, starting transfers between devices: 3.07 us -> 2.31 us  [passed_to(): lax.ppermute(x, 'tile', [(i, t % devices) for i, t in pairs if t is not N...]
  transfers between devices with their start and end apart: 12 -> 11, of which waited for: 7 -> 6; matrix products, arithmetic and copies ran while one was open for 0% -> 0% of each run, Pallas kernels for 20% -> 25%
where the time goes in v1:
time: 58 us; the launch traced here: 57.3 us
  Pallas kernels  19.7 us (34%)
  waiting for transfers between devices  19.7 us (34%)
  starting transfers between devices  17.5 us (30%)
    ppermute x8, starting transfers between devices, passed_along(): lax.ppermute(x, axis, [(i, (i + by) % devices) for i in range(devices)])  15.2 us
    ppermute x8, waiting for transfers between devices, passed_along(): lax.ppermute(x, axis, [(i, (i + by) % devices) for i in range(devices)])  12.3 us
    pallas_call x1, Pallas kernels, early_blocks(): pl.pallas_call(early_kernel, out_shape=[shape(1, BLOCKS, 3, SIDE, SIDE),...  7.73 us
    ppermute x3, waiting for transfers between devices, passed_to(): lax.ppermute(x, 'tile', [(i, t % devices) for i, t in pairs if t is not N...  7.4 us
    pallas_call x1, Pallas kernels, prepare(): pl.pallas_call(prepare_kernel, out_shape=[shape(3, SIDE, SIDE)] * 2 + [sh...  3.68 us
    pallas_call x1, Pallas kernels, late_blocks(): pl.pallas_call(late_kernel, out_shape=shape(1, BLOCKS, 3, SIDE, SIDE), in...  3 us
    ppermute x3, starting transfers between devices, passed_to(): lax.ppermute(x, 'tile', [(i, t % devices) for i, t in pairs if t is not N...  2.31 us
    pallas_call x1, Pallas kernels, lay_inflow(): pl.pallas_call(inflow_kernel, out_shape=[shape(BLOCKS, SIDE, SIDE), shape...  2.11 us
  transfers between devices with their start and end apart: 11, of which 6 were waited for; matrix products, arithmetic and copies ran while one was open for 0% of the time, Pallas kernels for 25%

profile of v1, /device:TPU:4, one launch (start us, length us, event | category | flops | bytes accessed | tf_op | source)
XLA Modules:
  0.0 57.3 jit_solution(15005287525958869225)
XLA Ops:
  0.0 2.1 %shard_map.74 = (f32[3,256,256]{2,1,0:T(8,128)S(1)}, f32[3,256,256]{2,1,0:T(8,128)S(1)}) custom-call(s32[1,128]{1,0:T(1,128)} %dest.9, f32[1,4,3,256,256]{4,3,2,1,0:T(8,128)} %state.3), custom_call_target="tpu_custom_call" | custom-call | tf_op jit(solution)/shard_map/pallas_call | solution.py:107
  2.1 0.1 collective-permute-start.2
  2.2 0.0 copy-start.3
  2.2 0.0 copy-start.4
  2.2 2.0 %collective-permute-start.8 = (f32[3,256,256]{2,1,0:T(8,128)S(1)}, f32[3,256,256]{2,1,0:T(8,128)S(1)}, u32[]{:S(2)}, u32[]{:S(2)}) collective-permute-start(f32[3,256,256]{2,1,0:T(8,128)S(1)} %get-tuple-element.38.block_a), channel_id=1, source_target_pairs={{0,8},{4,12},{8,16},{12,20},{16,24},{20,28},{24,32},{28,36},{32,40... | collective-permute-start | bytes 2359304 | tf_op jit(solution)/shard_map/ppermute | solution.py:693
  4.2 3.7 %shard_map.75 = (f32[3,256,256]{2,1,0:T(8,128)S(1)}, f32[3,256,256]{2,1,0:T(8,128)S(1)}, f32[5,8,256]{2,1,0:T(8,128)S(1)}, f32[4,8,256]{2,1,0:T(8,128)S(1)}, f32...) custom-call(s32[1,128]{1,0:T(1,128)} %dest.9, ...), custom_call_target="tpu_custom_call" | custom-call | tf_op jit(solution)/shard_map/pallas_call | solution.py:208
  7.9 0.0 copy-start
  7.9 6.9 %collective-permute-start.3 = (f32[5,8,256]{2,1,0:T(8,128)S(1)}, f32[5,8,256]{2,1,0:T(8,128)S(1)}, u32[]{:S(2)}, u32[]{:S(2)}) collective-permute-start(f32[5,8,256]{2,1,0:T(8,128)S(1)} %get-tuple-element.45), channel_id=1, source_target_pairs={{0,124},{4,0},{8,4},{12,8},{16,12},{20,16},{24,20},{28,24},{32,28}... | collective-permute-start | bytes 122888 | tf_op jit(solution)/shard_map/ppermute | solution.py:693
  14.8 2.1 %shard_map.73 = (f32[4,256,256]{2,1,0:T(8,128)S(1)}, f32[3,8,256]{2,1,0:T(8,128)S(1)}) custom-call(s32[1,4,16]{2,1,0:T(4,128)S(1)} %copy-done.3, f32[1,4,16]{2,1,0:T(4,128)S(1)} %copy-done.4), custom_call_target="tpu_custom_call" | custom-call | tf_op jit(solution)/shard_map/pallas_call | solution.py:536
  17.0 0.1 collective-permute-start.4
  17.0 4.2 %collective-permute-start.5 = (f32[1,8,256]{2,1,0:T(8,128)S(1)}, f32[1,8,256]{2,1,0:T(8,128)S(1)}, u32[]{:S(2)}, u32[]{:S(2)}) collective-permute-start(f32[1,8,256]{2,1,0:T(8,128)S(1)} %get-tuple-element.47), channel_id=1, source_target_pairs={{0,16},{4,20},{8,24},{12,28},{16,32},{20,36},{24,40},{28,44},{32,4... | collective-permute-start | bytes 24584 | tf_op jit(solution)/shard_map/ppermute | solution.py:693
  21.2 5.6 %collective-permute-done.1.pack2.refs_3_ = f32[6,8,256]{2,1,0:T(8,128)S(1)} collective-permute-done((f32[6,8,256]{2,1,0:T(8,128)S(1)}, f32[6,8,256]{2,1,0:T(8,128)S(1)}, u32[]{:S(2)}, u32[]{:S(2)}) %collective-permute-start.1) | collective-permute-done | bytes 49184 | tf_op jit(solution)/shard_map/ppermute | solution.py:693
  26.8 2.8 %collective-permute-done.pack1.refs_2_.refs_13_ = f32[10,8,256]{2,1,0:T(8,128)S(1)} collective-permute-done((f32[10,8,256]{2,1,0:T(8,128)S(1)}, f32[10,8,256]{2,1,0:T(8,128)S(1)}, u32[]{:S(2)}, u32[]{:S(2)}) %collective-permute-start) | collective-permute-done | bytes 81952 | tf_op jit(solution)/shard_map/ppermute | solution.py:693
  29.6 1.9 %collective-permute-start.9 = (f32[3,256,256]{2,1,0:T(8,128)S(1)}, f32[3,256,256]{2,1,0:T(8,128)S(1)}, u32[]{:S(2)}, u32[]{:S(2)}) collective-permute-start(f32[3,256,256]{2,1,0:T(8,128)S(1)} %get-tuple-element.64.refs_23_), channel_id=1, source_target_pairs={{0,24},{8,32},{16,40},{24,16},{32,56},{40,64},{48,72},{56,48},{64,... | collective-permute-start | bytes 2359304 | tf_op jit(solution)/shard_map/ppermute | solution.py:699
  31.6 0.3 collective-permute-start.10
  31.9 1.1 %shard_map.77 = (f32[8,8,256]{2,1,0:T(8,128)S(1)}, f32[6,8,256]{2,1,0:T(8,128)S(1)}, f32[16,8,256]{2,1,0:T(8,128)S(1)}, f32[16,8,256]{2,1,0:T(8,128)S(1)}, f32[8...) custom-call(s32[1,128]{1,0:T(1,128)S(1)} %copy-done.2, ...), custom_call_target="tpu_custom_call" | custom-call | tf_op jit(solution)/shard_map/pallas_call | solution.py:348
  33.0 0.6 %collective-permute-start.6 = (f32[12,8,256]{2,1,0:T(8,128)S(1)}, f32[12,8,256]{2,1,0:T(8,128)S(1)}, u32[]{:S(2)}, u32[]{:S(2)}) collective-permute-start(f32[12,8,256]{2,1,0:T(8,128)S(1)} %get-tuple-element.58.refs_15_), channel_id=1, source_target_pairs={{0,3},{1,0},{2,1},{3,2},{4,7},{5,4},{6,5},{7,6},{8,11},{9,8},{10,9... | collective-permute-start | bytes 294920 | tf_op jit(solution)/shard_map/ppermute | solution.py:693
  33.6 1.5 %collective-permute-start.7 = (f32[12,8,256]{2,1,0:T(8,128)S(1)}, f32[12,8,256]{2,1,0:T(8,128)S(1)}, u32[]{:S(2)}, u32[]{:S(2)}) collective-permute-start(f32[12,8,256]{2,1,0:T(8,128)S(1)} %get-tuple-element.59.refs_16_), channel_id=1, source_target_pairs={{0,1},{1,2},{2,3},{3,0},{4,5},{5,6},{6,7},{7,4},{8,9},{9,10},{10,1... | collective-permute-start | bytes 294920 | tf_op jit(solution)/shard_map/ppermute | solution.py:693
  35.0 3.1 %collective-permute-done.6.refs_17_ = f32[12,8,256]{2,1,0:T(8,128)S(1)} collective-permute-done((f32[12,8,256]{2,1,0:T(8,128)S(1)}, f32[12,8,256]{2,1,0:T(8,128)S(1)}, u32[]{:S(2)}, u32[]{:S(2)}) %collective-permute-start.6) | collective-permute-done | bytes 98336 | tf_op jit(solution)/shard_map/ppermute | solution.py:693
  38.1 0.9 %collective-permute-done.7.refs_18_ = f32[12,8,256]{2,1,0:T(8,128)S(1)} collective-permute-done((f32[12,8,256]{2,1,0:T(8,128)S(1)}, f32[12,8,256]{2,1,0:T(8,128)S(1)}, u32[]{:S(2)}, u32[]{:S(2)}) %collective-permute-start.7) | collective-permute-done | bytes 98336 | tf_op jit(solution)/shard_map/ppermute | solution.py:693
  39.0 6.7 %collective-permute-done.9.refs_24_ = f32[3,256,256]{2,1,0:T(8,128)S(1)} collective-permute-done((f32[3,256,256]{2,1,0:T(8,128)S(1)}, f32[3,256,256]{2,1,0:T(8,128)S(1)}, u32[]{:S(2)}, u32[]{:S(2)}) %collective-permute-start.9) | collective-permute-done | bytes 786464 | tf_op jit(solution)/shard_map/ppermute | solution.py:699
  45.6 7.7 %shard_map.79 = (f32[1,4,3,256,256]{4,3,2,1,0:T(8,128)}, f32[4,256,128]{2,1,0:T(8,128)S(1)}, f32[4,8,256]{2,1,0:T(8,128)S(1)}) custom-call(s32[1,128]{1,0:T(1,128)S(1)} %copy-done.2, s32[1,4,4]{2,1,0:T(4,128)S(1)} %copy-done.1, s32[1,4]{1,0:T(1,128)S(1)} %copy-done.5, f32[3,8,256]{2,1,0:T(8,128)S(1)} %get-tuple-element.37.refs_4_.edge_spill.refs_2_, ...), custom_call_target="tpu_custom_call" | custom-call | tf_op jit(solution)/shard_map/pallas_call | solution.py:649
  53.4 0.7 %collective-permute-done.10.arrived_x = f32[3,256,256]{2,1,0:T(8,128)S(1)} collective-permute-done((f32[3,256,256]{2,1,0:T(8,128)S(1)}, f32[3,256,256]{2,1,0:T(8,128)S(1)}, u32[]{:S(2)}, u32[]{:S(2)}) %collective-permute-start.10) | collective-permute-done | bytes 786464 | tf_op jit(solution)/shard_map/ppermute | solution.py:699
  54.1 3.0 %shard_map.80 = f32[1,4,3,256,256]{4,3,2,1,0:T(8,128)} custom-call(s32[1,128]{1,0:T(1,128)S(1)} %copy-done.2, s32[1,4]{1,0:T(1,128)S(1)} %copy-done.5, f32[1,4,2,256,256]{4,3,2,1,0:T(8,128)S(1)} %copy-done, f32[4,256,128]{2,1,0:T(8,128)S(1)} %get-tuple-element.65.columns, f32[4,8,256]{2,1,0:T(8,128)S(1)} %get-tuple-element.66.rows, ...), custom_call_target="tpu_custom_call", output_to_operand_aliasing={{}: (7, {})} | custom-call | tf_op jit(solution)/shard_map/pallas_call | solution.py:679
  (18 shorter events, 0.1 us)
Async XLA Ops:
  2.1 14.9 %collective-permute-start.2 = (f32[3,256,256]{2,1,0:T(8,128)S(1)}, f32[3,256,256]{2,1,0:T(8,128)S(1)}, u32[]{:S(2)}, u32[]{:S(2)}) collective-permute-start(f32[3,256,256]{2,1,0:T(8,128)S(1)} %get-tuple-element.39.block_w), channel_id=1, source_target_pairs={{0,4},{4,24},{8,12},{12,0},{16,20},{20,8},{24,28},{28,16},{32,36},... | collective-permute-start | bytes 2359304 | tf_op jit(solution)/shard_map/ppermute | solution.py:699
  2.2 12.6 %copy-start.3 = (s32[1,4,16]{2,1,0:T(4,128)S(1)}, s32[1,4,16]{2,1,0:T(4,128)}, u32[]{:S(2)}) copy-start(s32[1,4,16]{2,1,0:T(4,128)} %cells.3) | copy-start | bytes 772
  2.2 12.6 %copy-start.4 = (f32[1,4,16]{2,1,0:T(4,128)S(1)}, f32[1,4,16]{2,1,0:T(4,128)}, u32[]{:S(2)}) copy-start(f32[1,4,16]{2,1,0:T(4,128)} %rates.3) | copy-start | bytes 772
  2.2 27.4 %collective-permute-start.8 = (f32[3,256,256]{2,1,0:T(8,128)S(1)}, f32[3,256,256]{2,1,0:T(8,128)S(1)}, u32[]{:S(2)}, u32[]{:S(2)}) collective-permute-start(f32[3,256,256]{2,1,0:T(8,128)S(1)} %get-tuple-element.38.block_a), channel_id=1, source_target_pairs={{0,8},{4,12},{8,16},{12,20},{16,24},{20,28},{24,32},{28,36},{32,40... | collective-permute-start | bytes 2359304 | tf_op jit(solution)/shard_map/ppermute | solution.py:693
  7.9 24.0 %copy-start.1 = (s32[1,4,4]{2,1,0:T(4,128)S(1)}, s32[1,4,4]{2,1,0:T(4,128)}, u32[]{:S(2)}) copy-start(s32[1,4,4]{2,1,0:T(4,128)} %refs_0_.1) | copy-start | bytes 196
  7.9 24.0 %copy-start.2 = (s32[1,128]{1,0:T(1,128)S(1)}, s32[1,128]{1,0:T(1,128)}, u32[]{:S(2)}) copy-start(s32[1,128]{1,0:T(1,128)} %dest.9) | copy-start | bytes 1540
  7.9 37.7 %copy-start = (f32[1,4,2,256,256]{4,3,2,1,0:T(8,128)S(1)}, f32[1,4,2,256,256]{4,3,2,1,0:T(8,128)}, u32[]{:S(2)}) copy-start(f32[1,4,2,256,256]{4,3,2,1,0:T(8,128)} %terrain.1) | copy-start | bytes 6291460
  7.9 37.7 %copy-start.5 = (s32[1,4]{1,0:T(1,128)S(1)}, s32[1,4]{1,0:T(1,128)}, u32[]{:S(2)}) copy-start(s32[1,4]{1,0:T(1,128)} %wet.1) | copy-start | bytes 52
  7.9 9.0 %collective-permute-start.3 = (f32[5,8,256]{2,1,0:T(8,128)S(1)}, f32[5,8,256]{2,1,0:T(8,128)S(1)}, u32[]{:S(2)}, u32[]{:S(2)}) collective-permute-start(f32[5,8,256]{2,1,0:T(8,128)S(1)} %get-tuple-element.45), channel_id=1, source_target_pairs={{0,124},{4,0},{8,4},{12,8},{16,12},{20,16},{24,20},{28,24},{32,28}... | collective-permute-start | bytes 122888 | tf_op jit(solution)/shard_map/ppermute | solution.py:693
  14.8 14.8 %collective-permute-start = (f32[10,8,256]{2,1,0:T(8,128)S(1)}, f32[10,8,256]{2,1,0:T(8,128)S(1)}, u32[]{:S(2)}, u32[]{:S(2)}) collective-permute-start(f32[10,8,256]{2,1,0:T(8,128)S(1)} %get-tuple-element.41), channel_id=1, source_target_pairs={{0,4},{4,8},{8,12},{12,16},{16,20},{20,24},{24,28},{28,32},{32,36}... | collective-permute-start | bytes 245768 | tf_op jit(solution)/shard_map/ppermute | solution.py:693
  14.8 12.0 %collective-permute-start.1 = (f32[6,8,256]{2,1,0:T(8,128)S(1)}, f32[6,8,256]{2,1,0:T(8,128)S(1)}, u32[]{:S(2)}, u32[]{:S(2)}) collective-permute-start(f32[6,8,256]{2,1,0:T(8,128)S(1)} %get-tuple-element.42), channel_id=1, source_target_pairs={{0,8},{4,12},{8,16},{12,20},{16,24},{20,28},{24,32},{28,36},{32,40... | collective-permute-start | bytes 147464 | tf_op jit(solution)/shard_map/ppermute | solution.py:693
  17.0 12.7 %collective-permute-start.4 = (f32[5,8,256]{2,1,0:T(8,128)S(1)}, f32[5,8,256]{2,1,0:T(8,128)S(1)}, u32[]{:S(2)}, u32[]{:S(2)}) collective-permute-start(f32[5,8,256]{2,1,0:T(8,128)S(1)} %get-tuple-element.46), channel_id=1, source_target_pairs={{0,12},{4,16},{8,20},{12,24},{16,28},{20,32},{24,36},{28,40},{32,4... | collective-permute-start | bytes 122888 | tf_op jit(solution)/shard_map/ppermute | solution.py:693
  17.0 12.6 %collective-permute-start.5 = (f32[1,8,256]{2,1,0:T(8,128)S(1)}, f32[1,8,256]{2,1,0:T(8,128)S(1)}, u32[]{:S(2)}, u32[]{:S(2)}) collective-permute-start(f32[1,8,256]{2,1,0:T(8,128)S(1)} %get-tuple-element.47), channel_id=1, source_target_pairs={{0,16},{4,20},{8,24},{12,28},{16,32},{20,36},{24,40},{28,44},{32,4... | collective-permute-start | bytes 24584 | tf_op jit(solution)/shard_map/ppermute | solution.py:693
  29.6 16.0 %collective-permute-start.9 = (f32[3,256,256]{2,1,0:T(8,128)S(1)}, f32[3,256,256]{2,1,0:T(8,128)S(1)}, u32[]{:S(2)}, u32[]{:S(2)}) collective-permute-start(f32[3,256,256]{2,1,0:T(8,128)S(1)} %get-tuple-element.64.refs_23_), channel_id=1, source_target_pairs={{0,24},{8,32},{16,40},{24,16},{32,56},{40,64},{48,72},{56,48},{64,... | collective-permute-start | bytes 2359304 | tf_op jit(solution)/shard_map/ppermute | solution.py:699
  31.6 22.6 %collective-permute-start.10 = (f32[3,256,256]{2,1,0:T(8,128)S(1)}, f32[3,256,256]{2,1,0:T(8,128)S(1)}, u32[]{:S(2)}, u32[]{:S(2)}) collective-permute-start(f32[3,256,256]{2,1,0:T(8,128)S(1)} %get-tuple-element.67), channel_id=1, source_target_pairs={{0,12},{4,8},{8,20},{12,16},{16,28},{20,24},{24,36},{28,32},{32,44... | collective-permute-start | bytes 2359304 | tf_op jit(solution)/shard_map/ppermute | solution.py:699
  33.0 5.2 %collective-permute-start.6 = (f32[12,8,256]{2,1,0:T(8,128)S(1)}, f32[12,8,256]{2,1,0:T(8,128)S(1)}, u32[]{:S(2)}, u32[]{:S(2)}) collective-permute-start(f32[12,8,256]{2,1,0:T(8,128)S(1)} %get-tuple-element.58.refs_15_), channel_id=1, source_target_pairs={{0,3},{1,0},{2,1},{3,2},{4,7},{5,4},{6,5},{7,6},{8,11},{9,8},{10,9... | collective-permute-start | bytes 294920 | tf_op jit(solution)/shard_map/ppermute | solution.py:693
  33.6 5.4 %collective-permute-start.7 = (f32[12,8,256]{2,1,0:T(8,128)S(1)}, f32[12,8,256]{2,1,0:T(8,128)S(1)}, u32[]{:S(2)}, u32[]{:S(2)}) collective-permute-start(f32[12,8,256]{2,1,0:T(8,128)S(1)} %get-tuple-element.59.refs_16_), channel_id=1, source_target_pairs={{0,1},{1,2},{2,3},{3,0},{4,5},{5,6},{6,7},{7,4},{8,9},{9,10},{10,1... | collective-permute-start | bytes 294920 | tf_op jit(solution)/shard_map/ppermute | solution.py:693

commit v2 on v1

--- a/solution.py
+++ b/solution.py
@@ -278,8 +278,8 @@
 
 
 def arrange_kernel(
-    dest, entries, pack0, pack1, pack2, pack3, pack4, pack_back, ground_low, ground_high, edge_spill,
-    low, high, wide_low, wide_high, has_low, has_high, far_east, far_west, to_south, to_north,
+    dest, entries, pack0, pack1, pack2, pack3, pack4, pack_back, ground_low, ground_high, edge_spill, _key, _,
+    _relay, low, high, wide_low, wide_high, has_low, has_high, far_east, far_west, to_south, to_north,
     west, east,
 ):
     for out in (low, high, wide_low, wide_high, has_low, has_high):
@@ -343,17 +343,18 @@
         to_south[8 + b] = passed
 
 
-def arrange(dest, entries, packs, ground, edge_spill):
+def arrange(dest, entries, packs, ground, edge_spill, key, relay):
     outs = [(8, 8), (6, 8), (16, 8), (16, 8), (8,), (8,), (BLOCKS, 8), (BLOCKS, 8), (3 * BLOCKS, 8), (3 * BLOCKS, 8)]
     return pl.pallas_call(
         arrange_kernel,
-        out_shape=[shape(*dims, SIDE) for dims in outs],
-        in_specs=[SMEM] * 2 + [VMEM] * 9,
-        out_specs=[VMEM] * len(outs),
+        out_shape=[shape(3, SIDE, SIDE)] + [shape(*dims, SIDE) for dims in outs],
+        in_specs=[SMEM] * 2 + [VMEM] * 9 + [ANY] * 2,
+        out_specs=[ANY] + [VMEM] * len(outs),
+        input_output_aliases={12: 0},
         scratch_shapes=[pltpu.VMEM((BLOCKS, 8, SIDE), F32)] * 2,
         compiler_params=params(4),
         cost_estimate=cost(0, 0),
-    )(dest, entries, *packs, *ground, edge_spill)
+    )(dest, entries, *packs, *ground, edge_spill, key, relay)
 
 
 def along_edge(h, z, rough, flow, face_before, face_first, face_last):
@@ -630,27 +631,30 @@
     return [pltpu.VMEM((3, SIDE, SIDE), F32)] * 3 + [pltpu.SemaphoreType.DMA((SIDE // ROWS,))] * 2
 
 
-def early_kernel(dest, *refs):
+def blocks_kernel(dest, *refs):
     ins, refs = refs[:EDGE_INPUTS], refs[EDGE_INPUTS:]
-    terrain, spill, own, arrived_a, arrived_w, relayed, out, columns, rows = refs[:9]
-    edge_scratch, (then, done1, done2, sems1, sems2) = refs[9 : 9 + EDGE_SCRATCH], refs[9 + EDGE_SCRATCH :]
+    terrain, spill, own, arrived_a, arrived_x, arrived_w, relayed, out = refs[:8]
+    edge_scratch, (columns, rows, then, done1, done2, sems1, sems2) = refs[8 : 8 + EDGE_SCRATCH], refs[8 + EDGE_SCRATCH :]
     edges_kernel(*ins, columns, rows, *edge_scratch)
     shared = (dest, ins[1], terrain, columns, rows, spill)
     copies = block(OWN_SHIFTS, *shared, (own,), out, then, done1, sems1)
     later = block(A_SHIFTS, *shared, (arrived_a,), out, then, done2, sems2)
     for copy in copies:
         copy.wait()
-    later += block(W_SHIFTS, *shared, (arrived_w, relayed), out, then, done1, sems1)
+    copies = block(W_SHIFTS, *shared, (arrived_w, relayed), out, then, done1, sems1)
     for copy in later:
         copy.wait()
-
-
-def early_blocks(dest, edge_inputs, terrain, spill, own, arrived_a, arrived_w, relayed):
+    copies += block(X_SHIFTS, *shared, (arrived_x,), out, then, done2, sems2)
+    for copy in copies:
+        copy.wait()
+
+
+def all_blocks(dest, edge_inputs, terrain, spill, own, arrived_a, arrived_x, arrived_w, relayed):
     return pl.pallas_call(
-        early_kernel,
-        out_shape=[shape(1, BLOCKS, 3, SIDE, SIDE), shape(BLOCKS, SIDE, HALF), shape(BLOCKS, 8, SIDE)],
-        in_specs=[SMEM] * 3 + [VMEM] * (EDGE_INPUTS - 2 + 4) + [ANY] * 2,
-        out_specs=[HBM, VMEM, VMEM],
+        blocks_kernel,
+        out_shape=shape(1, BLOCKS, 3, SIDE, SIDE),
+        in_specs=[SMEM] * 3 + [VMEM] * (EDGE_INPUTS - 2 + 5) + [ANY] * 2,
+        out_specs=HBM,
         scratch_shapes=[
             pltpu.VMEM((16, 8, SIDE), F32),
             pltpu.VMEM((16, 8, SIDE), F32),
@@ -662,30 +666,13 @@
             pltpu.VMEM((2, 8, SIDE), F32),
             pltpu.VMEM((2, 8, 8, SIDE), F32),
             pltpu.VMEM((HALF, SIDE), F32),
+            pltpu.VMEM((BLOCKS, SIDE, HALF), F32),
+            pltpu.VMEM((BLOCKS, 8, SIDE), F32),
         ]
         + block_scratch(),
         compiler_params=params(16),
         cost_estimate=cost(0, 0),
-    )(dest, *edge_inputs, terrain, spill, own, arrived_a, arrived_w, relayed)
-
-
-def late_kernel(dest, wet, terrain, columns, rows, spill, arrived_x, _, out, then, done, sems):
-    shared = (dest, wet, terrain, columns, rows, spill)
-    for copy in block(X_SHIFTS, *shared, (arrived_x,), out, then, done, sems):
-        copy.wait()
-
-
-def late_blocks(dest, wet, terrain, columns, rows, spill, arrived_x, out):
-    return pl.pallas_call(
-        late_kernel,
-        out_shape=shape(1, BLOCKS, 3, SIDE, SIDE),
-        in_specs=[SMEM] * 2 + [VMEM] * 5 + [HBM],
-        out_specs=HBM,
-        input_output_aliases={7: 0},
-        scratch_shapes=[pltpu.VMEM((3, SIDE, SIDE), F32)] * 2 + [pltpu.SemaphoreType.DMA((SIDE // ROWS,))],
-        compiler_params=params(16),
-        cost_estimate=cost(0, 0),
-    )(dest, wet, terrain, columns, rows, spill, arrived_x, out)
+    )(dest, *edge_inputs, terrain, spill, own, arrived_a, arrived_x, arrived_w, relayed)
 
 
 def passed_along(x, axis, by, wrap=True):
@@ -731,22 +718,21 @@
     packs[1:3] = [passed_along(packs[d], "tile", d) for d in (1, 2)]
     packs[3], packs[4], arrived_w = gate((packs[3], packs[4], arrived_w), (packs[5], edge_spill))
     packs[3:5] = [passed_along(packs[d], "tile", d) for d in (3, 4)]
-    block_x, arrived_w = gate((block_x, arrived_w), (*packs[1:5], arrived_a))
+    (block_x,) = gate((block_x,), (arrived_a,))
     arrived_x = passed_to(block_x, next_chip_swapped)
+    arrived_w, low, high, wide_low, wide_high, has_low, has_high, far_east, far_west, to_south, to_north = arrange(
+        destination, neighbours, packs, ground, edge_spill, arrived_a, arrived_w
+    )
     relayed = passed_to(arrived_w, second_leg)
-    low, high, wide_low, wide_high, has_low, has_high, far_east, far_west, to_south, to_north = arrange(
-        destination, neighbours, packs, ground, edge_spill
-    )
     from_north = passed_along(to_south, "grp", -1)
     from_south = passed_along(to_north, "grp", 1)
     edge_inputs = (
         neighbours, wet_mask, edge_spill, low, high, *ground, wide_low, wide_high, has_low, has_high,
         far_east, far_west, packs[1], packs[5], to_south, to_north, from_north, from_south,
     )
-    out, columns, rows = early_blocks(
-        destination, edge_inputs, terrain, spill, own, arrived_a, arrived_w, relayed
-    )
-    return late_blocks(destination, wet_mask, terrain, columns, rows, spill, arrived_x, out)
+    return all_blocks(
+        destination, edge_inputs, terrain, spill, own, arrived_a, arrived_x, arrived_w, relayed
+    )
 
 
 def solution(mesh):

time: 58 us -> 59.3 us (1.022)
  the two profiles are of different devices: /device:TPU:4 before, /device:TPU:1 now
where the time goes in v2:
time: 59.3 us; the launch traced here: 59.1 us
  waiting for transfers between devices  24.4 us (41%)
  Pallas kernels  18.2 us (31%)
  starting transfers between devices  16.2 us (27%)
    ppermute x8, waiting for transfers between devices, passed_along(): lax.ppermute(x, axis, [(i, (i + by) % devices) for i in range(devices)])  13.8 us
    ppermute x3, waiting for transfers between devices, passed_to(): lax.ppermute(x, 'tile', [(i, t % devices) for i, t in pairs if t is not N...  10.6 us
    ppermute x8, starting transfers between devices, passed_along(): lax.ppermute(x, axis, [(i, (i + by) % devices) for i in range(devices)])  10.3 us
    pallas_call x1, Pallas kernels, all_blocks(): pl.pallas_call(blocks_kernel, out_shape=shape(1, BLOCKS, 3, SIDE, SIDE),...  9.26 us
    ppermute x3, starting transfers between devices, passed_to(): lax.ppermute(x, 'tile', [(i, t % devices) for i, t in pairs if t is not N...  5.93 us
    pallas_call x1, Pallas kernels, prepare(): pl.pallas_call(prepare_kernel, out_shape=[shape(3, SIDE, SIDE)] * 2 + [sh...  3.68 us
    pallas_call x1, Pallas kernels, lay_inflow(): pl.pallas_call(inflow_kernel, out_shape=[shape(BLOCKS, SIDE, SIDE), shape...  2.11 us
    pallas_call x1, Pallas kernels, pick_early(): pl.pallas_call(pick_kernel, out_shape=[shape(3, SIDE, SIDE)] * 2, in_spec...  2.08 us
  transfers between devices with their start and end apart: 11, of which 6 were waited for; matrix products, arithmetic and copies ran while one was open for 0% of the time, Pallas kernels for 12%

profile of v2, /device:TPU:1, one launch (start us, length us, event | category | flops | bytes accessed | tf_op | source)
XLA Modules:
  0.0 59.1 jit_solution(9916847539235847468)
XLA Ops:
  0.0 2.1 %shard_map.74 = (f32[3,256,256]{2,1,0:T(8,128)S(1)}, f32[3,256,256]{2,1,0:T(8,128)S(1)}) custom-call(s32[1,128]{1,0:T(1,128)} %dest.7, f32[1,4,3,256,256]{4,3,2,1,0:T(8,128)} %state.3), custom_call_target="tpu_custom_call" | custom-call | tf_op jit(solution)/shard_map/pallas_call | solution.py:107
  2.1 5.2 %collective-permute-start.2 = (f32[3,256,256]{2,1,0:T(8,128)S(1)}, f32[3,256,256]{2,1,0:T(8,128)S(1)}, u32[]{:S(2)}, u32[]{:S(2)}) collective-permute-start(f32[3,256,256]{2,1,0:T(8,128)S(1)} %get-tuple-element.35.block_w), channel_id=1, source_target_pairs={{0,4},{4,24},{8,12},{12,0},{16,20},{20,8},{24,28},{28,16},{32,36},... | collective-permute-start | bytes 2359304 | tf_op jit(solution)/shard_map/ppermute | solution.py:686
  7.3 3.7 %shard_map.75 = (f32[3,256,256]{2,1,0:T(8,128)S(1)}, f32[3,256,256]{2,1,0:T(8,128)S(1)}, f32[5,8,256]{2,1,0:T(8,128)S(1)}, f32[4,8,256]{2,1,0:T(8,128)S(1)}, f32...) custom-call(s32[1,128]{1,0:T(1,128)} %dest.7, ...), custom_call_target="tpu_custom_call" | custom-call | tf_op jit(solution)/shard_map/pallas_call | solution.py:208
  11.0 0.0 copy-start.1
  11.0 0.0 copy-start.4
  11.0 0.0 copy-start
  11.0 0.0 copy-start.5
  11.1 0.1 collective-permute-start.3
  11.1 1.7 %collective-permute-start = (f32[10,8,256]{2,1,0:T(8,128)S(1)}, f32[10,8,256]{2,1,0:T(8,128)S(1)}, u32[]{:S(2)}, u32[]{:S(2)}) collective-permute-start(f32[10,8,256]{2,1,0:T(8,128)S(1)} %get-tuple-element.37), channel_id=1, source_target_pairs={{0,4},{4,8},{8,12},{12,16},{16,20},{20,24},{24,28},{28,32},{32,36}... | collective-permute-start | bytes 245768 | tf_op jit(solution)/shard_map/ppermute | solution.py:680
  12.9 2.1 %shard_map.73 = (f32[4,256,256]{2,1,0:T(8,128)S(1)}, f32[3,8,256]{2,1,0:T(8,128)S(1)}) custom-call(s32[1,4,16]{2,1,0:T(4,128)S(1)} %copy-done.2, f32[1,4,16]{2,1,0:T(4,128)S(1)} %copy-done.3), custom_call_target="tpu_custom_call" | custom-call | tf_op jit(solution)/shard_map/pallas_call | solution.py:537
  15.0 0.0 collective-permute-done.3.refs_3_.pack_back.refs_14_
  15.0 1.2 %collective-permute-done.2.refs_2_ = f32[3,256,256]{2,1,0:T(8,128)S(1)} collective-permute-done((f32[3,256,256]{2,1,0:T(8,128)S(1)}, f32[3,256,256]{2,1,0:T(8,128)S(1)}, u32[]{:S(2)}, u32[]{:S(2)}) %collective-permute-start.2) | collective-permute-done | bytes 786464 | tf_op jit(solution)/shard_map/ppermute | solution.py:686
  16.2 2.8 %collective-permute-start.4 = (f32[5,8,256]{2,1,0:T(8,128)S(1)}, f32[5,8,256]{2,1,0:T(8,128)S(1)}, u32[]{:S(2)}, u32[]{:S(2)}) collective-permute-start(f32[5,8,256]{2,1,0:T(8,128)S(1)} %get-tuple-element.42), channel_id=1, source_target_pairs={{0,12},{4,16},{8,20},{12,24},{16,28},{20,32},{24,36},{28,40},{32,4... | collective-permute-start | bytes 122888 | tf_op jit(solution)/shard_map/ppermute | solution.py:680
  19.0 3.1 %collective-permute-start.5 = (f32[1,8,256]{2,1,0:T(8,128)S(1)}, f32[1,8,256]{2,1,0:T(8,128)S(1)}, u32[]{:S(2)}, u32[]{:S(2)}) collective-permute-start(f32[1,8,256]{2,1,0:T(8,128)S(1)} %get-tuple-element.43), channel_id=1, source_target_pairs={{0,16},{4,20},{8,24},{12,28},{16,32},{20,36},{24,40},{28,44},{32,4... | collective-permute-start | bytes 24584 | tf_op jit(solution)/shard_map/ppermute | solution.py:680
  22.1 7.4 %collective-permute-done.6._key.refs_1_.refs_22_ = f32[3,256,256]{2,1,0:T(8,128)S(1)} collective-permute-done((f32[3,256,256]{2,1,0:T(8,128)S(1)}, f32[3,256,256]{2,1,0:T(8,128)S(1)}, u32[]{:S(2)}, u32[]{:S(2)}) %collective-permute-start.6) | collective-permute-done | bytes 786464 | tf_op jit(solution)/shard_map/ppermute | solution.py:680
  29.5 1.4 %collective-permute-done.1.pack2 = f32[6,8,256]{2,1,0:T(8,128)S(1)} collective-permute-done((f32[6,8,256]{2,1,0:T(8,128)S(1)}, f32[6,8,256]{2,1,0:T(8,128)S(1)}, u32[]{:S(2)}, u32[]{:S(2)}) %collective-permute-start.1) | collective-permute-done | bytes 49184 | tf_op jit(solution)/shard_map/ppermute | solution.py:680
  31.0 1.1 %shard_map.77 = (f32[3,256,256]{2,1,0:T(8,128)S(1)}, f32[8,8,256]{2,1,0:T(8,128)S(1)}, f32[6,8,256]{2,1,0:T(8,128)S(1)}, f32[16,8,256]{2,1,0:T(8,128)S(1)}, f32[...) custom-call(s32[1,128]{1,0:T(1,128)S(1)} %copy-done.4, ...), custom_call_target="tpu_custom_call", output_to_operand_aliasing={{0}: (12, {})} | custom-call | tf_op jit(solution)/shard_map/pallas_call | solution.py:348
  32.1 0.7 %collective-permute-start.10 = (f32[3,256,256]{2,1,0:T(8,128)S(1)}, f32[3,256,256]{2,1,0:T(8,128)S(1)}, u32[]{:S(2)}, u32[]{:S(2)}) collective-permute-start(f32[3,256,256]{2,1,0:T(8,128)S(1)} %get-tuple-element.60.refs_24_), channel_id=1, source_target_pairs={{0,24},{8,32},{16,40},{24,16},{32,56},{40,64},{48,72},{56,48},{64,... | collective-permute-start | bytes 2359304 | tf_op jit(solution)/shard_map/ppermute | solution.py:686
  32.8 2.5 %collective-permute-start.7 = (f32[12,8,256]{2,1,0:T(8,128)S(1)}, f32[12,8,256]{2,1,0:T(8,128)S(1)}, u32[]{:S(2)}, u32[]{:S(2)}) collective-permute-start(f32[12,8,256]{2,1,0:T(8,128)S(1)} %get-tuple-element.55.refs_15_), channel_id=1, source_target_pairs={{0,3},{1,0},{2,1},{3,2},{4,7},{5,4},{6,5},{7,6},{8,11},{9,8},{10,9... | collective-permute-start | bytes 294920 | tf_op jit(solution)/shard_map/ppermute | solution.py:680
  35.3 0.0 collective-permute-start.8
  35.3 1.6 %collective-permute-done.7.refs_17_ = f32[12,8,256]{2,1,0:T(8,128)S(1)} collective-permute-done((f32[12,8,256]{2,1,0:T(8,128)S(1)}, f32[12,8,256]{2,1,0:T(8,128)S(1)}, u32[]{:S(2)}, u32[]{:S(2)}) %collective-permute-start.7) | collective-permute-done | bytes 98336 | tf_op jit(solution)/shard_map/ppermute | solution.py:680
  37.0 3.3 %collective-permute-done.8.refs_18_ = f32[12,8,256]{2,1,0:T(8,128)S(1)} collective-permute-done((f32[12,8,256]{2,1,0:T(8,128)S(1)}, f32[12,8,256]{2,1,0:T(8,128)S(1)}, u32[]{:S(2)}, u32[]{:S(2)}) %collective-permute-start.8) | collective-permute-done | bytes 98336 | tf_op jit(solution)/shard_map/ppermute | solution.py:680
  40.3 9.4 %collective-permute-done.9.refs_23_ = f32[3,256,256]{2,1,0:T(8,128)S(1)} collective-permute-done((f32[3,256,256]{2,1,0:T(8,128)S(1)}, f32[3,256,256]{2,1,0:T(8,128)S(1)}, u32[]{:S(2)}, u32[]{:S(2)}) %collective-permute-start.9) | collective-permute-done | bytes 786464 | tf_op jit(solution)/shard_map/ppermute | solution.py:686
  49.7 9.3 %shard_map.79 = f32[1,4,3,256,256]{4,3,2,1,0:T(8,128)} custom-call(s32[1,128]{1,0:T(1,128)S(1)} %copy-done.4, s32[1,4,4]{2,1,0:T(4,128)S(1)} %copy-done.1, s32[1,4]{1,0:T(1,128)S(1)} %copy-done.5, f32[3,8,256]{2,1,0:T(8,128)S(1)} %get-tuple-element.33.refs_4_.edge_spill.refs_2_, f32[8,8,256]{2,1,0:T(8,128)S(1)} %get-tuple-element.47.refs_3_, ...), custom_call_target="tpu_custom_call" | custom-call | tf_op jit(solution)/shard_map/pallas_call | solution.py:653
  (17 shorter events, 0.0 us)
Async XLA Ops:
  2.1 14.2 %collective-permute-start.2 = (f32[3,256,256]{2,1,0:T(8,128)S(1)}, f32[3,256,256]{2,1,0:T(8,128)S(1)}, u32[]{:S(2)}, u32[]{:S(2)}) collective-permute-start(f32[3,256,256]{2,1,0:T(8,128)S(1)} %get-tuple-element.35.block_w), channel_id=1, source_target_pairs={{0,4},{4,24},{8,12},{12,0},{16,20},{20,8},{24,28},{28,16},{32,36},... | collective-permute-start | bytes 2359304 | tf_op jit(solution)/shard_map/ppermute | solution.py:686
  7.3 5.6 %copy-start.2 = (s32[1,4,16]{2,1,0:T(4,128)S(1)}, s32[1,4,16]{2,1,0:T(4,128)}, u32[]{:S(2)}) copy-start(s32[1,4,16]{2,1,0:T(4,128)} %cells.3) | copy-start | bytes 772
  7.3 5.6 %copy-start.3 = (f32[1,4,16]{2,1,0:T(4,128)S(1)}, f32[1,4,16]{2,1,0:T(4,128)}, u32[]{:S(2)}) copy-start(f32[1,4,16]{2,1,0:T(4,128)} %rates.3) | copy-start | bytes 772
  7.3 22.2 %collective-permute-start.6 = (f32[3,256,256]{2,1,0:T(8,128)S(1)}, f32[3,256,256]{2,1,0:T(8,128)S(1)}, u32[]{:S(2)}, u32[]{:S(2)}) collective-permute-start(f32[3,256,256]{2,1,0:T(8,128)S(1)} %get-tuple-element.34.block_a), channel_id=1, source_target_pairs={{0,8},{4,12},{8,16},{12,20},{16,24},{20,28},{24,32},{28,36},{32,40... | collective-permute-start | bytes 2359304 | tf_op jit(solution)/shard_map/ppermute | solution.py:680
  11.0 20.0 %copy-start.1 = (s32[1,4,4]{2,1,0:T(4,128)S(1)}, s32[1,4,4]{2,1,0:T(4,128)}, u32[]{:S(2)}) copy-start(s32[1,4,4]{2,1,0:T(4,128)} %refs_0_.1) | copy-start | bytes 196
  11.0 20.0 %copy-start.4 = (s32[1,128]{1,0:T(1,128)S(1)}, s32[1,128]{1,0:T(1,128)}, u32[]{:S(2)}) copy-start(s32[1,128]{1,0:T(1,128)} %dest.7) | copy-start | bytes 1540
  11.0 38.7 %copy-start = (f32[1,4,2,256,256]{4,3,2,1,0:T(8,128)S(1)}, f32[1,4,2,256,256]{4,3,2,1,0:T(8,128)}, u32[]{:S(2)}) copy-start(f32[1,4,2,256,256]{4,3,2,1,0:T(8,128)} %refs_19_.1) | copy-start | bytes 6291460
  11.0 38.6 %copy-start.5 = (s32[1,4]{1,0:T(1,128)S(1)}, s32[1,4]{1,0:T(1,128)}, u32[]{:S(2)}) copy-start(s32[1,4]{1,0:T(1,128)} %refs_1_.1) | copy-start | bytes 52
  11.1 4.0 %collective-permute-start.3 = (f32[5,8,256]{2,1,0:T(8,128)S(1)}, f32[5,8,256]{2,1,0:T(8,128)S(1)}, u32[]{:S(2)}, u32[]{:S(2)}) collective-permute-start(f32[5,8,256]{2,1,0:T(8,128)S(1)} %get-tuple-element.41), channel_id=1, source_target_pairs={{0,124},{4,0},{8,4},{12,8},{16,12},{20,16},{24,20},{28,24},{32,28}... | collective-permute-start | bytes 122888 | tf_op jit(solution)/shard_map/ppermute | solution.py:680
  11.1 19.8 %collective-permute-start = (f32[10,8,256]{2,1,0:T(8,128)S(1)}, f32[10,8,256]{2,1,0:T(8,128)S(1)}, u32[]{:S(2)}, u32[]{:S(2)}) collective-permute-start(f32[10,8,256]{2,1,0:T(8,128)S(1)} %get-tuple-element.37), channel_id=1, source_target_pairs={{0,4},{4,8},{8,12},{12,16},{16,20},{20,24},{24,28},{28,32},{32,36}... | collective-permute-start | bytes 245768 | tf_op jit(solution)/shard_map/ppermute | solution.py:680
  12.9 18.1 %collective-permute-start.1 = (f32[6,8,256]{2,1,0:T(8,128)S(1)}, f32[6,8,256]{2,1,0:T(8,128)S(1)}, u32[]{:S(2)}, u32[]{:S(2)}) collective-permute-start(f32[6,8,256]{2,1,0:T(8,128)S(1)} %get-tuple-element.38), channel_id=1, source_target_pairs={{0,8},{4,12},{8,16},{12,20},{16,24},{20,28},{24,32},{28,36},{32,40... | collective-permute-start | bytes 147464 | tf_op jit(solution)/shard_map/ppermute | solution.py:680
  16.2 14.7 %collective-permute-start.4 = (f32[5,8,256]{2,1,0:T(8,128)S(1)}, f32[5,8,256]{2,1,0:T(8,128)S(1)}, u32[]{:S(2)}, u32[]{:S(2)}) collective-permute-start(f32[5,8,256]{2,1,0:T(8,128)S(1)} %get-tuple-element.42), channel_id=1, source_target_pairs={{0,12},{4,16},{8,20},{12,24},{16,28},{20,32},{24,36},{28,40},{32,4... | collective-permute-start | bytes 122888 | tf_op jit(solution)/shard_map/ppermute | solution.py:680
  19.0 12.0 %collective-permute-start.5 = (f32[1,8,256]{2,1,0:T(8,128)S(1)}, f32[1,8,256]{2,1,0:T(8,128)S(1)}, u32[]{:S(2)}, u32[]{:S(2)}) collective-permute-start(f32[1,8,256]{2,1,0:T(8,128)S(1)} %get-tuple-element.43), channel_id=1, source_target_pairs={{0,16},{4,20},{8,24},{12,28},{16,32},{20,36},{24,40},{28,44},{32,4... | collective-permute-start | bytes 24584 | tf_op jit(solution)/shard_map/ppermute | solution.py:680
  29.5 20.1 %collective-permute-start.9 = (f32[3,256,256]{2,1,0:T(8,128)S(1)}, f32[3,256,256]{2,1,0:T(8,128)S(1)}, u32[]{:S(2)}, u32[]{:S(2)}) collective-permute-start(f32[3,256,256]{2,1,0:T(8,128)S(1)} %shard_map.78), channel_id=1, source_target_pairs={{0,12},{4,8},{8,20},{12,16},{16,28},{20,24},{24,36},{28,32},{32,44... | collective-permute-start | bytes 2359304 | tf_op jit(solution)/shard_map/ppermute | solution.py:686
  32.1 17.6 %collective-permute-start.10 = (f32[3,256,256]{2,1,0:T(8,128)S(1)}, f32[3,256,256]{2,1,0:T(8,128)S(1)}, u32[]{:S(2)}, u32[]{:S(2)}) collective-permute-start(f32[3,256,256]{2,1,0:T(8,128)S(1)} %get-tuple-element.60.refs_24_), channel_id=1, source_target_pairs={{0,24},{8,32},{16,40},{24,16},{32,56},{40,64},{48,72},{56,48},{64,... | collective-permute-start | bytes 2359304 | tf_op jit(solution)/shard_map/ppermute | solution.py:686
  32.8 4.2 %collective-permute-start.7 = (f32[12,8,256]{2,1,0:T(8,128)S(1)}, f32[12,8,256]{2,1,0:T(8,128)S(1)}, u32[]{:S(2)}, u32[]{:S(2)}) collective-permute-start(f32[12,8,256]{2,1,0:T(8,128)S(1)} %get-tuple-element.55.refs_15_), channel_id=1, source_target_pairs={{0,3},{1,0},{2,1},{3,2},{4,7},{5,4},{6,5},{7,6},{8,11},{9,8},{10,9... | collective-permute-start | bytes 294920 | tf_op jit(solution)/shard_map/ppermute | solution.py:680
  35.3 5.0 %collective-permute-start.8 = (f32[12,8,256]{2,1,0:T(8,128)S(1)}, f32[12,8,256]{2,1,0:T(8,128)S(1)}, u32[]{:S(2)}, u32[]{:S(2)}) collective-permute-start(f32[12,8,256]{2,1,0:T(8,128)S(1)} %get-tuple-element.56.refs_16_), channel_id=1, source_target_pairs={{0,1},{1,2},{2,3},{3,0},{4,5},{5,6},{6,7},{7,4},{8,9},{9,10},{10,1... | collective-permute-start | bytes 294920 | tf_op jit(solution)/shard_map/ppermute | solution.py:680

commit v3 on v2

--- a/solution.py
+++ b/solution.py
@@ -716,9 +716,11 @@
     spill, edge_spill = lay_inflow(inflow_cells, inflow_rates)
     packs[5] = passed_along(packs[5], "tile", -1)
     packs[1:3] = [passed_along(packs[d], "tile", d) for d in (1, 2)]
-    packs[3], packs[4], arrived_w = gate((packs[3], packs[4], arrived_w), (packs[5], edge_spill))
-    packs[3:5] = [passed_along(packs[d], "tile", d) for d in (3, 4)]
-    (block_x,) = gate((block_x,), (arrived_a,))
+    (packs[3],) = gate((packs[3],), (packs[5], edge_spill))
+    packs[3] = passed_along(packs[3], "tile", 3)
+    (packs[4],) = gate((packs[4],), (arrived_a,))
+    packs[4] = passed_along(packs[4], "tile", 4)
+    block_x, arrived_w = gate((block_x, arrived_w), (arrived_a,))
     arrived_x = passed_to(block_x, next_chip_swapped)
     arrived_w, low, high, wide_low, wide_high, has_low, has_high, far_east, far_west, to_south, to_north = arrange(
         destination, neighbours, packs, ground, edge_spill, arrived_a, arrived_w

time: 59.3 us -> 61.6 us (1.039)
  the two profiles are of different devices: /device:TPU:1 before, /device:TPU:4 now
where the time goes in v3:
time: 61.6 us; the launch traced here: 61.3 us
  waiting for transfers between devices  30.3 us (49%)
  Pallas kernels  18.2 us (30%)
  starting transfers between devices  12.5 us (20%)
    ppermute x8, waiting for transfers between devices, passed_along(): lax.ppermute(x, axis, [(i, (i + by) % devices) for i in range(devices)])  21.4 us
    ppermute x8, starting transfers between devices, passed_along(): lax.ppermute(x, axis, [(i, (i + by) % devices) for i in range(devices)])  10.5 us
    pallas_call x1, Pallas kernels, all_blocks(): pl.pallas_call(blocks_kernel, out_shape=shape(1, BLOCKS, 3, SIDE, SIDE),...  9.24 us
    ppermute x3, waiting for transfers between devices, passed_to(): lax.ppermute(x, 'tile', [(i, t % devices) for i, t in pairs if t is not N...  8.84 us
    pallas_call x1, Pallas kernels, prepare(): pl.pallas_call(prepare_kernel, out_shape=[shape(3, SIDE, SIDE)] * 2 + [sh...  3.68 us
    pallas_call x1, Pallas kernels, lay_inflow(): pl.pallas_call(inflow_kernel, out_shape=[shape(BLOCKS, SIDE, SIDE), shape...  2.11 us
    pallas_call x1, Pallas kernels, pick_early(): pl.pallas_call(pick_kernel, out_shape=[shape(3, SIDE, SIDE)] * 2, in_spec...  2.08 us
    ppermute x3, starting transfers between devices, passed_to(): lax.ppermute(x, 'tile', [(i, t % devices) for i, t in pairs if t is not N...  2 us
  transfers between devices with their start and end apart: 11, of which 7 were waited for; matrix products, arithmetic and copies ran while one was open for 0% of the time, Pallas kernels for 11%

profile of v3, /device:TPU:4, one launch (start us, length us, event | category | flops | bytes accessed | tf_op | source)
XLA Modules:
  0.0 61.3 jit_solution(8046017719184265955)
XLA Ops:
  0.0 2.1 %shard_map.74 = (f32[3,256,256]{2,1,0:T(8,128)S(1)}, f32[3,256,256]{2,1,0:T(8,128)S(1)}) custom-call(s32[1,128]{1,0:T(1,128)} %dest.7, f32[1,4,3,256,256]{4,3,2,1,0:T(8,128)} %state.3), custom_call_target="tpu_custom_call" | custom-call | tf_op jit(solution)/shard_map/pallas_call | solution.py:107
  2.1 2.0 %collective-permute-start.4 = (f32[3,256,256]{2,1,0:T(8,128)S(1)}, f32[3,256,256]{2,1,0:T(8,128)S(1)}, u32[]{:S(2)}, u32[]{:S(2)}) collective-permute-start(f32[3,256,256]{2,1,0:T(8,128)S(1)} %get-tuple-element.33.block_a), channel_id=1, source_target_pairs={{0,8},{4,12},{8,16},{12,20},{16,24},{20,28},{24,32},{28,36},{32,40... | collective-permute-start | bytes 2359304 | tf_op jit(solution)/shard_map/ppermute | solution.py:680
  4.1 0.0 collective-permute-start.6
  4.1 3.7 %shard_map.75 = (f32[3,256,256]{2,1,0:T(8,128)S(1)}, f32[3,256,256]{2,1,0:T(8,128)S(1)}, f32[5,8,256]{2,1,0:T(8,128)S(1)}, f32[4,8,256]{2,1,0:T(8,128)S(1)}, f32...) custom-call(s32[1,128]{1,0:T(1,128)} %dest.7, ...), custom_call_target="tpu_custom_call" | custom-call | tf_op jit(solution)/shard_map/pallas_call | solution.py:208
  7.8 0.0 copy-start.1
  7.8 0.0 copy-start.4
  7.8 0.0 copy-start
  7.8 0.0 copy-start.5
  7.8 6.4 %collective-permute-start.2 = (f32[5,8,256]{2,1,0:T(8,128)S(1)}, f32[5,8,256]{2,1,0:T(8,128)S(1)}, u32[]{:S(2)}, u32[]{:S(2)}) collective-permute-start(f32[5,8,256]{2,1,0:T(8,128)S(1)} %get-tuple-element.39), channel_id=1, source_target_pairs={{0,124},{4,0},{8,4},{12,8},{16,12},{20,16},{24,20},{28,24},{32,28}... | collective-permute-start | bytes 122888 | tf_op jit(solution)/shard_map/ppermute | solution.py:680
  14.2 2.1 %shard_map.73 = (f32[4,256,256]{2,1,0:T(8,128)S(1)}, f32[3,8,256]{2,1,0:T(8,128)S(1)}) custom-call(s32[1,4,16]{2,1,0:T(4,128)S(1)} %copy-done.2, f32[1,4,16]{2,1,0:T(4,128)S(1)} %copy-done.3), custom_call_target="tpu_custom_call" | custom-call | tf_op jit(solution)/shard_map/pallas_call | solution.py:537
  16.4 0.1 collective-permute-start.3
  16.4 11.0 %collective-permute-done.4.refs_1_.refs_2_._key.refs_22_ = f32[3,256,256]{2,1,0:T(8,128)S(1)} collective-permute-done((f32[3,256,256]{2,1,0:T(8,128)S(1)}, f32[3,256,256]{2,1,0:T(8,128)S(1)}, u32[]{:S(2)}, u32[]{:S(2)}) %collective-permute-start.4) | collective-permute-done | bytes 786464 | tf_op jit(solution)/shard_map/ppermute | solution.py:680
  27.5 0.1 collective-permute-start.9
  27.5 1.0 %collective-permute-done.1.pack2 = f32[6,8,256]{2,1,0:T(8,128)S(1)} collective-permute-done((f32[6,8,256]{2,1,0:T(8,128)S(1)}, f32[6,8,256]{2,1,0:T(8,128)S(1)}, u32[]{:S(2)}, u32[]{:S(2)}) %collective-permute-start.1) | collective-permute-done | bytes 49184 | tf_op jit(solution)/shard_map/ppermute | solution.py:680
  28.5 6.3 %collective-permute-done.5.pack4 = f32[1,8,256]{2,1,0:T(8,128)S(1)} collective-permute-done((f32[1,8,256]{2,1,0:T(8,128)S(1)}, f32[1,8,256]{2,1,0:T(8,128)S(1)}, u32[]{:S(2)}, u32[]{:S(2)}) %collective-permute-start.5) | collective-permute-done | bytes 8224 | tf_op jit(solution)/shard_map/ppermute | solution.py:680
  34.9 1.1 %shard_map.79 = (f32[3,256,256]{2,1,0:T(8,128)S(1)}, f32[8,8,256]{2,1,0:T(8,128)S(1)}, f32[6,8,256]{2,1,0:T(8,128)S(1)}, f32[16,8,256]{2,1,0:T(8,128)S(1)}, f32[...) custom-call(s32[1,128]{1,0:T(1,128)S(1)} %copy-done.4, ...), custom_call_target="tpu_custom_call", output_to_operand_aliasing={{0}: (12, {})} | custom-call | tf_op jit(solution)/shard_map/pallas_call | solution.py:348
  35.9 1.9 %collective-permute-start.10 = (f32[3,256,256]{2,1,0:T(8,128)S(1)}, f32[3,256,256]{2,1,0:T(8,128)S(1)}, u32[]{:S(2)}, u32[]{:S(2)}) collective-permute-start(f32[3,256,256]{2,1,0:T(8,128)S(1)} %get-tuple-element.58.refs_24_), channel_id=1, source_target_pairs={{0,24},{8,32},{16,40},{24,16},{32,56},{40,64},{48,72},{56,48},{64,... | collective-permute-start | bytes 2359304 | tf_op jit(solution)/shard_map/ppermute | solution.py:686
  37.9 0.6 collective-permute-start.7
  38.5 1.5 %collective-permute-start.8 = (f32[12,8,256]{2,1,0:T(8,128)S(1)}, f32[12,8,256]{2,1,0:T(8,128)S(1)}, u32[]{:S(2)}, u32[]{:S(2)}) collective-permute-start(f32[12,8,256]{2,1,0:T(8,128)S(1)} %get-tuple-element.54.refs_16_), channel_id=1, source_target_pairs={{0,1},{1,2},{2,3},{3,0},{4,5},{5,6},{6,7},{7,4},{8,9},{9,10},{10,1... | collective-permute-start | bytes 294920 | tf_op jit(solution)/shard_map/ppermute | solution.py:680
  40.0 2.6 %collective-permute-done.7.refs_17_ = f32[12,8,256]{2,1,0:T(8,128)S(1)} collective-permute-done((f32[12,8,256]{2,1,0:T(8,128)S(1)}, f32[12,8,256]{2,1,0:T(8,128)S(1)}, u32[]{:S(2)}, u32[]{:S(2)}) %collective-permute-start.7) | collective-permute-done | bytes 98336 | tf_op jit(solution)/shard_map/ppermute | solution.py:680
  42.6 0.5 collective-permute-done.8.refs_18_
  43.1 6.0 %collective-permute-done.9.refs_23_ = f32[3,256,256]{2,1,0:T(8,128)S(1)} collective-permute-done((f32[3,256,256]{2,1,0:T(8,128)S(1)}, f32[3,256,256]{2,1,0:T(8,128)S(1)}, u32[]{:S(2)}, u32[]{:S(2)}) %collective-permute-start.9) | collective-permute-done | bytes 786464 | tf_op jit(solution)/shard_map/ppermute | solution.py:686
  49.1 2.8 %collective-permute-done.10.refs_25_ = f32[3,256,256]{2,1,0:T(8,128)S(1)} collective-permute-done((f32[3,256,256]{2,1,0:T(8,128)S(1)}, f32[3,256,256]{2,1,0:T(8,128)S(1)}, u32[]{:S(2)}, u32[]{:S(2)}) %collective-permute-start.10) | collective-permute-done | bytes 786464 | tf_op jit(solution)/shard_map/ppermute | solution.py:686
  51.9 9.2 %shard_map.80 = f32[1,4,3,256,256]{4,3,2,1,0:T(8,128)} custom-call(s32[1,128]{1,0:T(1,128)S(1)} %copy-done.4, s32[1,4,4]{2,1,0:T(4,128)S(1)} %copy-done.1, s32[1,4]{1,0:T(1,128)S(1)} %copy-done.5, f32[3,8,256]{2,1,0:T(8,128)S(1)} %get-tuple-element.32.refs_2_.edge_spill, f32[8,8,256]{2,1,0:T(8,128)S(1)} %get-tuple-element.45.refs_3_, ...), custom_call_target="tpu_custom_call" | custom-call | tf_op jit(solution)/shard_map/pallas_call | solution.py:653
  (18 shorter events, 0.0 us)
Async XLA Ops:
  2.1 25.4 %collective-permute-start.4 = (f32[3,256,256]{2,1,0:T(8,128)S(1)}, f32[3,256,256]{2,1,0:T(8,128)S(1)}, u32[]{:S(2)}, u32[]{:S(2)}) collective-permute-start(f32[3,256,256]{2,1,0:T(8,128)S(1)} %get-tuple-element.33.block_a), channel_id=1, source_target_pairs={{0,8},{4,12},{8,16},{12,20},{16,24},{20,28},{24,32},{28,36},{32,40... | collective-permute-start | bytes 2359304 | tf_op jit(solution)/shard_map/ppermute | solution.py:680
  4.1 10.1 %copy-start.2 = (s32[1,4,16]{2,1,0:T(4,128)S(1)}, s32[1,4,16]{2,1,0:T(4,128)}, u32[]{:S(2)}) copy-start(s32[1,4,16]{2,1,0:T(4,128)} %cells.3) | copy-start | bytes 772
  4.1 10.1 %copy-start.3 = (f32[1,4,16]{2,1,0:T(4,128)S(1)}, f32[1,4,16]{2,1,0:T(4,128)}, u32[]{:S(2)}) copy-start(f32[1,4,16]{2,1,0:T(4,128)} %rates.3) | copy-start | bytes 772
  4.1 23.4 %collective-permute-start.6 = (f32[3,256,256]{2,1,0:T(8,128)S(1)}, f32[3,256,256]{2,1,0:T(8,128)S(1)}, u32[]{:S(2)}, u32[]{:S(2)}) collective-permute-start(f32[3,256,256]{2,1,0:T(8,128)S(1)} %get-tuple-element.34.block_w), channel_id=1, source_target_pairs={{0,4},{4,24},{8,12},{12,0},{16,20},{20,8},{24,28},{28,16},{32,36},... | collective-permute-start | bytes 2359304 | tf_op jit(solution)/shard_map/ppermute | solution.py:686
  7.8 27.1 %copy-start.1 = (s32[1,4,4]{2,1,0:T(4,128)S(1)}, s32[1,4,4]{2,1,0:T(4,128)}, u32[]{:S(2)}) copy-start(s32[1,4,4]{2,1,0:T(4,128)} %refs_0_.1) | copy-start | bytes 196
  7.8 27.1 %copy-start.4 = (s32[1,128]{1,0:T(1,128)S(1)}, s32[1,128]{1,0:T(1,128)}, u32[]{:S(2)}) copy-start(s32[1,128]{1,0:T(1,128)} %dest.7) | copy-start | bytes 1540
  7.8 44.1 %copy-start = (f32[1,4,2,256,256]{4,3,2,1,0:T(8,128)S(1)}, f32[1,4,2,256,256]{4,3,2,1,0:T(8,128)}, u32[]{:S(2)}) copy-start(f32[1,4,2,256,256]{4,3,2,1,0:T(8,128)} %refs_19_.1) | copy-start | bytes 6291460
  7.8 44.1 %copy-start.5 = (s32[1,4]{1,0:T(1,128)S(1)}, s32[1,4]{1,0:T(1,128)}, u32[]{:S(2)}) copy-start(s32[1,4]{1,0:T(1,128)} %refs_1_.1) | copy-start | bytes 52
  7.8 8.5 %collective-permute-start.2 = (f32[5,8,256]{2,1,0:T(8,128)S(1)}, f32[5,8,256]{2,1,0:T(8,128)S(1)}, u32[]{:S(2)}, u32[]{:S(2)}) collective-permute-start(f32[5,8,256]{2,1,0:T(8,128)S(1)} %get-tuple-element.39), channel_id=1, source_target_pairs={{0,124},{4,0},{8,4},{12,8},{16,12},{20,16},{24,20},{28,24},{32,28}... | collective-permute-start | bytes 122888 | tf_op jit(solution)/shard_map/ppermute | solution.py:680
  14.2 14.3 %collective-permute-start = (f32[10,8,256]{2,1,0:T(8,128)S(1)}, f32[10,8,256]{2,1,0:T(8,128)S(1)}, u32[]{:S(2)}, u32[]{:S(2)}) collective-permute-start(f32[10,8,256]{2,1,0:T(8,128)S(1)} %get-tuple-element.36), channel_id=1, source_target_pairs={{0,4},{4,8},{8,12},{12,16},{16,20},{20,24},{24,28},{28,32},{32,36}... | collective-permute-start | bytes 245768 | tf_op jit(solution)/shard_map/ppermute | solution.py:680
  14.2 14.3 %collective-permute-start.1 = (f32[6,8,256]{2,1,0:T(8,128)S(1)}, f32[6,8,256]{2,1,0:T(8,128)S(1)}, u32[]{:S(2)}, u32[]{:S(2)}) collective-permute-start(f32[6,8,256]{2,1,0:T(8,128)S(1)} %get-tuple-element.37), channel_id=1, source_target_pairs={{0,8},{4,12},{8,16},{12,20},{16,24},{20,28},{24,32},{28,36},{32,40... | collective-permute-start | bytes 147464 | tf_op jit(solution)/shard_map/ppermute | solution.py:680
  16.4 12.1 %collective-permute-start.3 = (f32[5,8,256]{2,1,0:T(8,128)S(1)}, f32[5,8,256]{2,1,0:T(8,128)S(1)}, u32[]{:S(2)}, u32[]{:S(2)}) collective-permute-start(f32[5,8,256]{2,1,0:T(8,128)S(1)} %shard_map.76), channel_id=1, source_target_pairs={{0,12},{4,16},{8,20},{12,24},{16,28},{20,32},{24,36},{28,40},{32,4... | collective-permute-start | bytes 122888 | tf_op jit(solution)/shard_map/ppermute | solution.py:680
  27.5 7.4 %collective-permute-start.5 = (f32[1,8,256]{2,1,0:T(8,128)S(1)}, f32[1,8,256]{2,1,0:T(8,128)S(1)}, u32[]{:S(2)}, u32[]{:S(2)}) collective-permute-start(f32[1,8,256]{2,1,0:T(8,128)S(1)} %shard_map.77), channel_id=1, source_target_pairs={{0,16},{4,20},{8,24},{12,28},{16,32},{20,36},{24,40},{28,44},{32,4... | collective-permute-start | bytes 24584 | tf_op jit(solution)/shard_map/ppermute | solution.py:680
  27.5 21.7 %collective-permute-start.9 = (f32[3,256,256]{2,1,0:T(8,128)S(1)}, f32[3,256,256]{2,1,0:T(8,128)S(1)}, u32[]{:S(2)}, u32[]{:S(2)}) collective-permute-start(f32[3,256,256]{2,1,0:T(8,128)S(1)} %get-tuple-element.57), channel_id=1, source_target_pairs={{0,12},{4,8},{8,20},{12,16},{16,28},{20,24},{24,36},{28,32},{32,44... | collective-permute-start | bytes 2359304 | tf_op jit(solution)/shard_map/ppermute | solution.py:686
  35.9 16.0 %collective-permute-start.10 = (f32[3,256,256]{2,1,0:T(8,128)S(1)}, f32[3,256,256]{2,1,0:T(8,128)S(1)}, u32[]{:S(2)}, u32[]{:S(2)}) collective-permute-start(f32[3,256,256]{2,1,0:T(8,128)S(1)} %get-tuple-element.58.refs_24_), channel_id=1, source_target_pairs={{0,24},{8,32},{16,40},{24,16},{32,56},{40,64},{48,72},{56,48},{64,... | collective-permute-start | bytes 2359304 | tf_op jit(solution)/shard_map/ppermute | solution.py:686
  37.9 4.7 %collective-permute-start.7 = (f32[12,8,256]{2,1,0:T(8,128)S(1)}, f32[12,8,256]{2,1,0:T(8,128)S(1)}, u32[]{:S(2)}, u32[]{:S(2)}) collective-permute-start(f32[12,8,256]{2,1,0:T(8,128)S(1)} %get-tuple-element.53.refs_15_), channel_id=1, source_target_pairs={{0,3},{1,0},{2,1},{3,2},{4,7},{5,4},{6,5},{7,6},{8,11},{9,8},{10,9... | collective-permute-start | bytes 294920 | tf_op jit(solution)/shard_map/ppermute | solution.py:680
  38.5 4.6 %collective-permute-start.8 = (f32[12,8,256]{2,1,0:T(8,128)S(1)}, f32[12,8,256]{2,1,0:T(8,128)S(1)}, u32[]{:S(2)}, u32[]{:S(2)}) collective-permute-start(f32[12,8,256]{2,1,0:T(8,128)S(1)} %get-tuple-element.54.refs_16_), channel_id=1, source_target_pairs={{0,1},{1,2},{2,3},{3,0},{4,5},{5,6},{6,7},{7,4},{8,9},{9,10},{10,1... | collective-permute-start | bytes 294920 | tf_op jit(solution)/shard_map/ppermute | solution.py:680

commit v4 on v1

--- a/solution.py
+++ b/solution.py
@@ -632,24 +632,21 @@
 
 def early_kernel(dest, *refs):
     ins, refs = refs[:EDGE_INPUTS], refs[EDGE_INPUTS:]
-    terrain, spill, own, arrived_a, arrived_w, relayed, out, columns, rows = refs[:9]
-    edge_scratch, (then, done1, done2, sems1, sems2) = refs[9 : 9 + EDGE_SCRATCH], refs[9 + EDGE_SCRATCH :]
+    terrain, spill, own, arrived_a, out, columns, rows = refs[:7]
+    edge_scratch, (then, done1, done2, sems1, sems2) = refs[7 : 7 + EDGE_SCRATCH], refs[7 + EDGE_SCRATCH :]
     edges_kernel(*ins, columns, rows, *edge_scratch)
     shared = (dest, ins[1], terrain, columns, rows, spill)
     copies = block(OWN_SHIFTS, *shared, (own,), out, then, done1, sems1)
     later = block(A_SHIFTS, *shared, (arrived_a,), out, then, done2, sems2)
-    for copy in copies:
+    for copy in copies + later:
         copy.wait()
-    later += block(W_SHIFTS, *shared, (arrived_w, relayed), out, then, done1, sems1)
-    for copy in later:
-        copy.wait()
-
-
-def early_blocks(dest, edge_inputs, terrain, spill, own, arrived_a, arrived_w, relayed):
+
+
+def early_blocks(dest, edge_inputs, terrain, spill, own, arrived_a):
     return pl.pallas_call(
         early_kernel,
         out_shape=[shape(1, BLOCKS, 3, SIDE, SIDE), shape(BLOCKS, SIDE, HALF), shape(BLOCKS, 8, SIDE)],
-        in_specs=[SMEM] * 3 + [VMEM] * (EDGE_INPUTS - 2 + 4) + [ANY] * 2,
+        in_specs=[SMEM] * 3 + [VMEM] * (EDGE_INPUTS - 2 + 4),
         out_specs=[HBM, VMEM, VMEM],
         scratch_shapes=[
             pltpu.VMEM((16, 8, SIDE), F32),
@@ -666,26 +663,27 @@
         + block_scratch(),
         compiler_params=params(16),
         cost_estimate=cost(0, 0),
-    )(dest, *edge_inputs, terrain, spill, own, arrived_a, arrived_w, relayed)
-
-
-def late_kernel(dest, wet, terrain, columns, rows, spill, arrived_x, _, out, then, done, sems):
+    )(dest, *edge_inputs, terrain, spill, own, arrived_a)
+
+
+def late_kernel(shifts, dest, wet, terrain, columns, rows, spill, *refs):
+    out, then, done, sems = refs[-4:]
     shared = (dest, wet, terrain, columns, rows, spill)
-    for copy in block(X_SHIFTS, *shared, (arrived_x,), out, then, done, sems):
+    for copy in block(shifts, *shared, refs[:-5], out, then, done, sems):
         copy.wait()
 
 
-def late_blocks(dest, wet, terrain, columns, rows, spill, arrived_x, out):
+def late_block(shifts, dest, wet, terrain, columns, rows, spill, states, out):
     return pl.pallas_call(
-        late_kernel,
+        functools.partial(late_kernel, shifts),
         out_shape=shape(1, BLOCKS, 3, SIDE, SIDE),
-        in_specs=[SMEM] * 2 + [VMEM] * 5 + [HBM],
+        in_specs=[SMEM] * 2 + [VMEM] * 4 + [ANY if shifts == W_SHIFTS else VMEM] * len(states) + [HBM],
         out_specs=HBM,
-        input_output_aliases={7: 0},
+        input_output_aliases={6 + len(states): 0},
         scratch_shapes=[pltpu.VMEM((3, SIDE, SIDE), F32)] * 2 + [pltpu.SemaphoreType.DMA((SIDE // ROWS,))],
         compiler_params=params(16),
         cost_estimate=cost(0, 0),
-    )(dest, wet, terrain, columns, rows, spill, arrived_x, out)
+    )(dest, wet, terrain, columns, rows, spill, *states, out)
 
 
 def passed_along(x, axis, by, wrap=True):
@@ -743,10 +741,10 @@
         neighbours, wet_mask, edge_spill, low, high, *ground, wide_low, wide_high, has_low, has_high,
         far_east, far_west, packs[1], packs[5], to_south, to_north, from_north, from_south,
     )
-    out, columns, rows = early_blocks(
-        destination, edge_inputs, terrain, spill, own, arrived_a, arrived_w, relayed
-    )
-    return late_blocks(destination, wet_mask, terrain, columns, rows, spill, arrived_x, out)
+    out, columns, rows = early_blocks(destination, edge_inputs, terrain, spill, own, arrived_a)
+    shared = (destination, wet_mask, terrain, columns, rows, spill)
+    out = late_block(W_SHIFTS, *shared, (arrived_w, relayed), out)
+    return late_block(X_SHIFTS, *shared, (arrived_x,), out)
 
 
 def solution(mesh):

time: 58 us -> 58 us (level)
  Pallas kernels: 19.7 us -> 20.6 us
  waiting for transfers between devices: 19.7 us -> 18.8 us
    pallas_call x1 -> x2, Pallas kernels: 3 us -> 6.24 us  [late_block(): pl.pallas_call(functools.partial(late_kernel, shifts), out_shape=shape(1,...]
    pallas_call x1, Pallas kernels: 7.73 us -> 5.38 us  [early_blocks(): pl.pallas_call(early_kernel, out_shape=[shape(1, BLOCKS, 3, SIDE, SIDE),...]
    ppermute x3, waiting for transfers between devices: 7.4 us -> 6.51 us  [passed_to(): lax.ppermute(x, 'tile', [(i, t % devices) for i, t in pairs if t is not N...]
  transfers between devices with their start and end apart: 11 -> 11, of which waited for: 6 -> 6; matrix products, arithmetic and copies ran while one was open for 0% -> 0% of each run, Pallas kernels for 25% -> 27%
where the time goes in v4:
time: 58 us; the launch traced here: 57.3 us
  Pallas kernels  20.6 us (36%)
  waiting for transfers between devices  18.8 us (32%)
  starting transfers between devices  17.5 us (30%)
    ppermute x8, starting transfers between devices, passed_along(): lax.ppermute(x, axis, [(i, (i + by) % devices) for i in range(devices)])  15.2 us
    ppermute x8, waiting for transfers between devices, passed_along(): lax.ppermute(x, axis, [(i, (i + by) % devices) for i in range(devices)])  12.3 us
    ppermute x3, waiting for transfers between devices, passed_to(): lax.ppermute(x, 'tile', [(i, t % devices) for i, t in pairs if t is not N...  6.51 us
    pallas_call x2, Pallas kernels, late_block(): pl.pallas_call(functools.partial(late_kernel, shifts), out_shape=shape(1,...  6.24 us
    pallas_call x1, Pallas kernels, early_blocks(): pl.pallas_call(early_kernel, out_shape=[shape(1, BLOCKS, 3, SIDE, SIDE),...  5.38 us
    pallas_call x1, Pallas kernels, prepare(): pl.pallas_call(prepare_kernel, out_shape=[shape(3, SIDE, SIDE)] * 2 + [sh...  3.68 us
    ppermute x3, starting transfers between devices, passed_to(): lax.ppermute(x, 'tile', [(i, t % devices) for i, t in pairs if t is not N...  2.31 us
    pallas_call x1, Pallas kernels, lay_inflow(): pl.pallas_call(inflow_kernel, out_shape=[shape(BLOCKS, SIDE, SIDE), shape...  2.11 us
  transfers between devices with their start and end apart: 11, of which 6 were waited for; matrix products, arithmetic and copies ran while one was open for 0% of the time, Pallas kernels for 27%

profile of v4, /device:TPU:4, one launch (start us, length us, event | category | flops | bytes accessed | tf_op | source)
XLA Modules:
  0.0 57.3 jit_solution(7928748977905836022)
XLA Ops:
  0.0 2.1 %shard_map.74 = (f32[3,256,256]{2,1,0:T(8,128)S(1)}, f32[3,256,256]{2,1,0:T(8,128)S(1)}) custom-call(s32[1,128]{1,0:T(1,128)} %dest.11, f32[1,4,3,256,256]{4,3,2,1,0:T(8,128)} %state.3), custom_call_target="tpu_custom_call" | custom-call | tf_op jit(solution)/shard_map/pallas_call | solution.py:107
  2.1 0.1 collective-permute-start.2
  2.2 0.0 copy-start.3
  2.2 0.0 copy-start.4
  2.2 2.0 %collective-permute-start.8 = (f32[3,256,256]{2,1,0:T(8,128)S(1)}, f32[3,256,256]{2,1,0:T(8,128)S(1)}, u32[]{:S(2)}, u32[]{:S(2)}) collective-permute-start(f32[3,256,256]{2,1,0:T(8,128)S(1)} %get-tuple-element.38.block_a), channel_id=1, source_target_pairs={{0,8},{4,12},{8,16},{12,20},{16,24},{20,28},{24,32},{28,36},{32,40... | collective-permute-start | bytes 2359304 | tf_op jit(solution)/shard_map/ppermute | solution.py:691
  4.2 3.7 %shard_map.75 = (f32[3,256,256]{2,1,0:T(8,128)S(1)}, f32[3,256,256]{2,1,0:T(8,128)S(1)}, f32[5,8,256]{2,1,0:T(8,128)S(1)}, f32[4,8,256]{2,1,0:T(8,128)S(1)}, f32...) custom-call(s32[1,128]{1,0:T(1,128)} %dest.11, ...), custom_call_target="tpu_custom_call" | custom-call | tf_op jit(solution)/shard_map/pallas_call | solution.py:208
  7.9 6.9 %collective-permute-start.3 = (f32[5,8,256]{2,1,0:T(8,128)S(1)}, f32[5,8,256]{2,1,0:T(8,128)S(1)}, u32[]{:S(2)}, u32[]{:S(2)}) collective-permute-start(f32[5,8,256]{2,1,0:T(8,128)S(1)} %get-tuple-element.45), channel_id=1, source_target_pairs={{0,124},{4,0},{8,4},{12,8},{16,12},{20,16},{24,20},{28,24},{32,28}... | collective-permute-start | bytes 122888 | tf_op jit(solution)/shard_map/ppermute | solution.py:691
  14.8 2.1 %shard_map.73 = (f32[4,256,256]{2,1,0:T(8,128)S(1)}, f32[3,8,256]{2,1,0:T(8,128)S(1)}) custom-call(s32[1,4,16]{2,1,0:T(4,128)S(1)} %copy-done.3, f32[1,4,16]{2,1,0:T(4,128)S(1)} %copy-done.4), custom_call_target="tpu_custom_call" | custom-call | tf_op jit(solution)/shard_map/pallas_call | solution.py:536
  17.0 0.1 collective-permute-start.4
  17.0 4.2 %collective-permute-start.5 = (f32[1,8,256]{2,1,0:T(8,128)S(1)}, f32[1,8,256]{2,1,0:T(8,128)S(1)}, u32[]{:S(2)}, u32[]{:S(2)}) collective-permute-start(f32[1,8,256]{2,1,0:T(8,128)S(1)} %get-tuple-element.47), channel_id=1, source_target_pairs={{0,16},{4,20},{8,24},{12,28},{16,32},{20,36},{24,40},{28,44},{32,4... | collective-permute-start | bytes 24584 | tf_op jit(solution)/shard_map/ppermute | solution.py:691
  21.2 5.6 %collective-permute-done.1.pack2.refs_3_ = f32[6,8,256]{2,1,0:T(8,128)S(1)} collective-permute-done((f32[6,8,256]{2,1,0:T(8,128)S(1)}, f32[6,8,256]{2,1,0:T(8,128)S(1)}, u32[]{:S(2)}, u32[]{:S(2)}) %collective-permute-start.1) | collective-permute-done | bytes 49184 | tf_op jit(solution)/shard_map/ppermute | solution.py:691
  26.8 2.8 %collective-permute-done.pack1.refs_13_.refs_2_ = f32[10,8,256]{2,1,0:T(8,128)S(1)} collective-permute-done((f32[10,8,256]{2,1,0:T(8,128)S(1)}, f32[10,8,256]{2,1,0:T(8,128)S(1)}, u32[]{:S(2)}, u32[]{:S(2)}) %collective-permute-start) | collective-permute-done | bytes 81952 | tf_op jit(solution)/shard_map/ppermute | solution.py:691
  29.6 1.9 %collective-permute-start.10 = (f32[3,256,256]{2,1,0:T(8,128)S(1)}, f32[3,256,256]{2,1,0:T(8,128)S(1)}, u32[]{:S(2)}, u32[]{:S(2)}) collective-permute-start(f32[3,256,256]{2,1,0:T(8,128)S(1)} %get-tuple-element.67.refs_0_), channel_id=1, source_target_pairs={{0,24},{8,32},{16,40},{24,16},{32,56},{40,64},{48,72},{56,48},{64,... | collective-permute-start | bytes 2359304 | tf_op jit(solution)/shard_map/ppermute | solution.py:697
  31.6 0.3 collective-permute-start.9
  31.9 1.1 %shard_map.77 = (f32[8,8,256]{2,1,0:T(8,128)S(1)}, f32[6,8,256]{2,1,0:T(8,128)S(1)}, f32[16,8,256]{2,1,0:T(8,128)S(1)}, f32[16,8,256]{2,1,0:T(8,128)S(1)}, f32[8...) custom-call(s32[1,128]{1,0:T(1,128)S(1)} %copy-done.2, ...), custom_call_target="tpu_custom_call" | custom-call | tf_op jit(solution)/shard_map/pallas_call | solution.py:348
  33.0 0.6 %collective-permute-start.6 = (f32[12,8,256]{2,1,0:T(8,128)S(1)}, f32[12,8,256]{2,1,0:T(8,128)S(1)}, u32[]{:S(2)}, u32[]{:S(2)}) collective-permute-start(f32[12,8,256]{2,1,0:T(8,128)S(1)} %get-tuple-element.58.refs_15_), channel_id=1, source_target_pairs={{0,3},{1,0},{2,1},{3,2},{4,7},{5,4},{6,5},{7,6},{8,11},{9,8},{10,9... | collective-permute-start | bytes 294920 | tf_op jit(solution)/shard_map/ppermute | solution.py:691
  33.6 1.5 %collective-permute-start.7 = (f32[12,8,256]{2,1,0:T(8,128)S(1)}, f32[12,8,256]{2,1,0:T(8,128)S(1)}, u32[]{:S(2)}, u32[]{:S(2)}) collective-permute-start(f32[12,8,256]{2,1,0:T(8,128)S(1)} %get-tuple-element.59.refs_16_), channel_id=1, source_target_pairs={{0,1},{1,2},{2,3},{3,0},{4,5},{5,6},{6,7},{7,4},{8,9},{9,10},{10,1... | collective-permute-start | bytes 294920 | tf_op jit(solution)/shard_map/ppermute | solution.py:691
  35.0 3.1 %collective-permute-done.6.refs_17_ = f32[12,8,256]{2,1,0:T(8,128)S(1)} collective-permute-done((f32[12,8,256]{2,1,0:T(8,128)S(1)}, f32[12,8,256]{2,1,0:T(8,128)S(1)}, u32[]{:S(2)}, u32[]{:S(2)}) %collective-permute-start.6) | collective-permute-done | bytes 98336 | tf_op jit(solution)/shard_map/ppermute | solution.py:691
  38.1 0.9 %collective-permute-done.7.refs_18_ = f32[12,8,256]{2,1,0:T(8,128)S(1)} collective-permute-done((f32[12,8,256]{2,1,0:T(8,128)S(1)}, f32[12,8,256]{2,1,0:T(8,128)S(1)}, u32[]{:S(2)}, u32[]{:S(2)}) %collective-permute-start.7) | collective-permute-done | bytes 98336 | tf_op jit(solution)/shard_map/ppermute | solution.py:691
  39.0 5.4 %shard_map.78 = (f32[1,4,3,256,256]{4,3,2,1,0:T(8,128)}, f32[4,256,128]{2,1,0:T(8,128)S(1)}, f32[4,8,256]{2,1,0:T(8,128)S(1)}) custom-call(s32[1,128]{1,0:T(1,128)S(1)} %copy-done.2, s32[1,4,4]{2,1,0:T(4,128)S(1)} %copy-done.1, s32[1,4]{1,0:T(1,128)S(1)} %copy-done.5, f32[3,8,256]{2,1,0:T(8,128)S(1)} %get-tuple-element.37.refs_4_.edge_spill.refs_2_, ...), custom_call_target="tpu_custom_call" | custom-call | tf_op jit(solution)/shard_map/pallas_call | solution.py:646
  44.4 1.3 %collective-permute-done.10.refs_1_ = f32[3,256,256]{2,1,0:T(8,128)S(1)} collective-permute-done((f32[3,256,256]{2,1,0:T(8,128)S(1)}, f32[3,256,256]{2,1,0:T(8,128)S(1)}, u32[]{:S(2)}, u32[]{:S(2)}) %collective-permute-start.10) | collective-permute-done | bytes 786464 | tf_op jit(solution)/shard_map/ppermute | solution.py:697
  45.6 3.2 %shard_map.80.refs_1_ = f32[1,4,3,256,256]{4,3,2,1,0:T(8,128)} custom-call(s32[1,128]{1,0:T(1,128)S(1)} %copy-done.2, s32[1,4]{1,0:T(1,128)S(1)} %copy-done.5, f32[1,4,2,256,256]{4,3,2,1,0:T(8,128)S(1)} %copy-done, f32[4,256,128]{2,1,0:T(8,128)S(1)} %get-tuple-element.62.columns, ...), custom_call_target="tpu_custom_call", output_to_operand_aliasing={{}: (8, {})} | custom-call | tf_op jit(solution)/shard_map/pallas_call | solution.py:677
  48.9 5.2 %collective-permute-done.9.refs_0_ = f32[3,256,256]{2,1,0:T(8,128)S(1)} collective-permute-done((f32[3,256,256]{2,1,0:T(8,128)S(1)}, f32[3,256,256]{2,1,0:T(8,128)S(1)}, u32[]{:S(2)}, u32[]{:S(2)}) %collective-permute-start.9) | collective-permute-done | bytes 786464 | tf_op jit(solution)/shard_map/ppermute | solution.py:697
  54.1 3.0 %shard_map.81 = f32[1,4,3,256,256]{4,3,2,1,0:T(8,128)} custom-call(s32[1,128]{1,0:T(1,128)S(1)} %copy-done.2, s32[1,4]{1,0:T(1,128)S(1)} %copy-done.5, f32[1,4,2,256,256]{4,3,2,1,0:T(8,128)S(1)} %copy-done, f32[4,256,128]{2,1,0:T(8,128)S(1)} %get-tuple-element.62.columns, f32[4,8,256]{2,1,0:T(8,128)S(1)} %get-tuple-element.63.rows, ...), custom_call_target="tpu_custom_call", output_to_operand_aliasing={{}: (7, {})} | custom-call | tf_op jit(solution)/shard_map/pallas_call | solution.py:677
  (19 shorter events, 0.1 us)
Async XLA Ops:
  2.1 14.9 %collective-permute-start.2 = (f32[3,256,256]{2,1,0:T(8,128)S(1)}, f32[3,256,256]{2,1,0:T(8,128)S(1)}, u32[]{:S(2)}, u32[]{:S(2)}) collective-permute-start(f32[3,256,256]{2,1,0:T(8,128)S(1)} %get-tuple-element.39.block_w), channel_id=1, source_target_pairs={{0,4},{4,24},{8,12},{12,0},{16,20},{20,8},{24,28},{28,16},{32,36},... | collective-permute-start | bytes 2359304 | tf_op jit(solution)/shard_map/ppermute | solution.py:697
  2.2 12.6 %copy-start.3 = (s32[1,4,16]{2,1,0:T(4,128)S(1)}, s32[1,4,16]{2,1,0:T(4,128)}, u32[]{:S(2)}) copy-start(s32[1,4,16]{2,1,0:T(4,128)} %cells.3) | copy-start | bytes 772
  2.2 12.6 %copy-start.4 = (f32[1,4,16]{2,1,0:T(4,128)S(1)}, f32[1,4,16]{2,1,0:T(4,128)}, u32[]{:S(2)}) copy-start(f32[1,4,16]{2,1,0:T(4,128)} %rates.3) | copy-start | bytes 772
  2.2 27.4 %collective-permute-start.8 = (f32[3,256,256]{2,1,0:T(8,128)S(1)}, f32[3,256,256]{2,1,0:T(8,128)S(1)}, u32[]{:S(2)}, u32[]{:S(2)}) collective-permute-start(f32[3,256,256]{2,1,0:T(8,128)S(1)} %get-tuple-element.38.block_a), channel_id=1, source_target_pairs={{0,8},{4,12},{8,16},{12,20},{16,24},{20,28},{24,32},{28,36},{32,40... | collective-permute-start | bytes 2359304 | tf_op jit(solution)/shard_map/ppermute | solution.py:691
  7.9 24.0 %copy-start.1 = (s32[1,4,4]{2,1,0:T(4,128)S(1)}, s32[1,4,4]{2,1,0:T(4,128)}, u32[]{:S(2)}) copy-start(s32[1,4,4]{2,1,0:T(4,128)} %refs_0_.1) | copy-start | bytes 196
  7.9 24.0 %copy-start.2 = (s32[1,128]{1,0:T(1,128)S(1)}, s32[1,128]{1,0:T(1,128)}, u32[]{:S(2)}) copy-start(s32[1,128]{1,0:T(1,128)} %dest.11) | copy-start | bytes 1540
  7.9 31.1 %copy-start = (f32[1,4,2,256,256]{4,3,2,1,0:T(8,128)S(1)}, f32[1,4,2,256,256]{4,3,2,1,0:T(8,128)}, u32[]{:S(2)}) copy-start(f32[1,4,2,256,256]{4,3,2,1,0:T(8,128)} %terrain.3) | copy-start | bytes 6291460
  7.9 31.1 %copy-start.5 = (s32[1,4]{1,0:T(1,128)S(1)}, s32[1,4]{1,0:T(1,128)}, u32[]{:S(2)}) copy-start(s32[1,4]{1,0:T(1,128)} %wet.3) | copy-start | bytes 52
  7.9 9.0 %collective-permute-start.3 = (f32[5,8,256]{2,1,0:T(8,128)S(1)}, f32[5,8,256]{2,1,0:T(8,128)S(1)}, u32[]{:S(2)}, u32[]{:S(2)}) collective-permute-start(f32[5,8,256]{2,1,0:T(8,128)S(1)} %get-tuple-element.45), channel_id=1, source_target_pairs={{0,124},{4,0},{8,4},{12,8},{16,12},{20,16},{24,20},{28,24},{32,28}... | collective-permute-start | bytes 122888 | tf_op jit(solution)/shard_map/ppermute | solution.py:691
  14.8 14.8 %collective-permute-start = (f32[10,8,256]{2,1,0:T(8,128)S(1)}, f32[10,8,256]{2,1,0:T(8,128)S(1)}, u32[]{:S(2)}, u32[]{:S(2)}) collective-permute-start(f32[10,8,256]{2,1,0:T(8,128)S(1)} %get-tuple-element.41), channel_id=1, source_target_pairs={{0,4},{4,8},{8,12},{12,16},{16,20},{20,24},{24,28},{28,32},{32,36}... | collective-permute-start | bytes 245768 | tf_op jit(solution)/shard_map/ppermute | solution.py:691
  14.8 12.0 %collective-permute-start.1 = (f32[6,8,256]{2,1,0:T(8,128)S(1)}, f32[6,8,256]{2,1,0:T(8,128)S(1)}, u32[]{:S(2)}, u32[]{:S(2)}) collective-permute-start(f32[6,8,256]{2,1,0:T(8,128)S(1)} %get-tuple-element.42), channel_id=1, source_target_pairs={{0,8},{4,12},{8,16},{12,20},{16,24},{20,28},{24,32},{28,36},{32,40... | collective-permute-start | bytes 147464 | tf_op jit(solution)/shard_map/ppermute | solution.py:691
  17.0 12.7 %collective-permute-start.4 = (f32[5,8,256]{2,1,0:T(8,128)S(1)}, f32[5,8,256]{2,1,0:T(8,128)S(1)}, u32[]{:S(2)}, u32[]{:S(2)}) collective-permute-start(f32[5,8,256]{2,1,0:T(8,128)S(1)} %get-tuple-element.46), channel_id=1, source_target_pairs={{0,12},{4,16},{8,20},{12,24},{16,28},{20,32},{24,36},{28,40},{32,4... | collective-permute-start | bytes 122888 | tf_op jit(solution)/shard_map/ppermute | solution.py:691
  17.0 12.6 %collective-permute-start.5 = (f32[1,8,256]{2,1,0:T(8,128)S(1)}, f32[1,8,256]{2,1,0:T(8,128)S(1)}, u32[]{:S(2)}, u32[]{:S(2)}) collective-permute-start(f32[1,8,256]{2,1,0:T(8,128)S(1)} %get-tuple-element.47), channel_id=1, source_target_pairs={{0,16},{4,20},{8,24},{12,28},{16,32},{20,36},{24,40},{28,44},{32,4... | collective-permute-start | bytes 24584 | tf_op jit(solution)/shard_map/ppermute | solution.py:691
  29.6 16.0 %collective-permute-start.10 = (f32[3,256,256]{2,1,0:T(8,128)S(1)}, f32[3,256,256]{2,1,0:T(8,128)S(1)}, u32[]{:S(2)}, u32[]{:S(2)}) collective-permute-start(f32[3,256,256]{2,1,0:T(8,128)S(1)} %get-tuple-element.67.refs_0_), channel_id=1, source_target_pairs={{0,24},{8,32},{16,40},{24,16},{32,56},{40,64},{48,72},{56,48},{64,... | collective-permute-start | bytes 2359304 | tf_op jit(solution)/shard_map/ppermute | solution.py:697
  31.6 22.6 %collective-permute-start.9 = (f32[3,256,256]{2,1,0:T(8,128)S(1)}, f32[3,256,256]{2,1,0:T(8,128)S(1)}, u32[]{:S(2)}, u32[]{:S(2)}) collective-permute-start(f32[3,256,256]{2,1,0:T(8,128)S(1)} %get-tuple-element.66), channel_id=1, source_target_pairs={{0,12},{4,8},{8,20},{12,16},{16,28},{20,24},{24,36},{28,32},{32,44... | collective-permute-start | bytes 2359304 | tf_op jit(solution)/shard_map/ppermute | solution.py:697
  33.0 5.2 %collective-permute-start.6 = (f32[12,8,256]{2,1,0:T(8,128)S(1)}, f32[12,8,256]{2,1,0:T(8,128)S(1)}, u32[]{:S(2)}, u32[]{:S(2)}) collective-permute-start(f32[12,8,256]{2,1,0:T(8,128)S(1)} %get-tuple-element.58.refs_15_), channel_id=1, source_target_pairs={{0,3},{1,0},{2,1},{3,2},{4,7},{5,4},{6,5},{7,6},{8,11},{9,8},{10,9... | collective-permute-start | bytes 294920 | tf_op jit(solution)/shard_map/ppermute | solution.py:691
  33.6 5.4 %collective-permute-start.7 = (f32[12,8,256]{2,1,0:T(8,128)S(1)}, f32[12,8,256]{2,1,0:T(8,128)S(1)}, u32[]{:S(2)}, u32[]{:S(2)}) collective-permute-start(f32[12,8,256]{2,1,0:T(8,128)S(1)} %get-tuple-element.59.refs_16_), channel_id=1, source_target_pairs={{0,1},{1,2},{2,3},{3,0},{4,5},{5,6},{6,7},{7,4},{8,9},{9,10},{10,1... | collective-permute-start | bytes 294920 | tf_op jit(solution)/shard_map/ppermute | solution.py:691

commit v5 on v4

--- a/solution.py
+++ b/solution.py
@@ -727,9 +727,9 @@
     spill, edge_spill = lay_inflow(inflow_cells, inflow_rates)
     packs[5] = passed_along(packs[5], "tile", -1)
     packs[1:3] = [passed_along(packs[d], "tile", d) for d in (1, 2)]
-    packs[3], packs[4], arrived_w = gate((packs[3], packs[4], arrived_w), (packs[5], edge_spill))
+    packs[3], packs[4], arrived_w = gate((packs[3], packs[4], arrived_w), (packs[5],))
     packs[3:5] = [passed_along(packs[d], "tile", d) for d in (3, 4)]
-    block_x, arrived_w = gate((block_x, arrived_w), (*packs[1:5], arrived_a))
+    block_x, arrived_w = gate((block_x, arrived_w), (*packs[1:5], arrived_a, edge_spill))
     arrived_x = passed_to(block_x, next_chip_swapped)
     relayed = passed_to(arrived_w, second_leg)
     low, high, wide_low, wide_high, has_low, has_high, far_east, far_west, to_south, to_north = arrange(

time: 58 us -> 58 us (level)
  transfers between devices with their start and end apart: 11 -> 11, of which waited for: 6 -> 7; matrix products, arithmetic and copies ran while one was open for 0% -> 0% of each run, Pallas kernels for 27% -> 27%
where the time goes in v5:
time: 58 us; the launch traced here: 57.3 us
  Pallas kernels  20.6 us (36%)
  waiting for transfers between devices  18.9 us (33%)
  starting transfers between devices  17.6 us (30%)
    ppermute x8, starting transfers between devices, passed_along(): lax.ppermute(x, axis, [(i, (i + by) % devices) for i in range(devices)])  15.2 us
    ppermute x8, waiting for transfers between devices, passed_along(): lax.ppermute(x, axis, [(i, (i + by) % devices) for i in range(devices)])  12.4 us
    ppermute x3, waiting for transfers between devices, passed_to(): lax.ppermute(x, 'tile', [(i, t % devices) for i, t in pairs if t is not N...  6.45 us
    pallas_call x2, Pallas kernels, late_block(): pl.pallas_call(functools.partial(late_kernel, shifts), out_shape=shape(1,...  6.24 us
    pallas_call x1, Pallas kernels, early_blocks(): pl.pallas_call(early_kernel, out_shape=[shape(1, BLOCKS, 3, SIDE, SIDE),...  5.38 us
    pallas_call x1, Pallas kernels, prepare(): pl.pallas_call(prepare_kernel, out_shape=[shape(3, SIDE, SIDE)] * 2 + [sh...  3.68 us
    ppermute x3, starting transfers between devices, passed_to(): lax.ppermute(x, 'tile', [(i, t % devices) for i, t in pairs if t is not N...  2.37 us
    pallas_call x1, Pallas kernels, lay_inflow(): pl.pallas_call(inflow_kernel, out_shape=[shape(BLOCKS, SIDE, SIDE), shape...  2.11 us
  transfers between devices with their start and end apart: 11, of which 7 were waited for; matrix products, arithmetic and copies ran while one was open for 0% of the time, Pallas kernels for 27%

profile of v5, /device:TPU:4, one launch (start us, length us, event | category | flops | bytes accessed | tf_op | source)
XLA Modules:
  0.0 57.3 jit_solution(10241032043056000343)
XLA Ops:
  0.0 2.1 %shard_map.74 = (f32[3,256,256]{2,1,0:T(8,128)S(1)}, f32[3,256,256]{2,1,0:T(8,128)S(1)}) custom-call(s32[1,128]{1,0:T(1,128)} %dest.11, f32[1,4,3,256,256]{4,3,2,1,0:T(8,128)} %state.3), custom_call_target="tpu_custom_call" | custom-call | tf_op jit(solution)/shard_map/pallas_call | solution.py:107
  2.1 0.1 collective-permute-start.2
  2.2 0.0 copy-start.4
  2.2 2.0 %collective-permute-start.8 = (f32[3,256,256]{2,1,0:T(8,128)S(1)}, f32[3,256,256]{2,1,0:T(8,128)S(1)}, u32[]{:S(2)}, u32[]{:S(2)}) collective-permute-start(f32[3,256,256]{2,1,0:T(8,128)S(1)} %get-tuple-element.38.block_a), channel_id=1, source_target_pairs={{0,8},{4,12},{8,16},{12,20},{16,24},{20,28},{24,32},{28,36},{32,40... | collective-permute-start | bytes 2359304 | tf_op jit(solution)/shard_map/ppermute | solution.py:691
  4.2 3.7 %shard_map.75 = (f32[3,256,256]{2,1,0:T(8,128)S(1)}, f32[3,256,256]{2,1,0:T(8,128)S(1)}, f32[5,8,256]{2,1,0:T(8,128)S(1)}, f32[4,8,256]{2,1,0:T(8,128)S(1)}, f32...) custom-call(s32[1,128]{1,0:T(1,128)} %dest.11, ...), custom_call_target="tpu_custom_call" | custom-call | tf_op jit(solution)/shard_map/pallas_call | solution.py:208
  7.9 0.0 copy-start
  7.9 6.9 %collective-permute-start.3 = (f32[5,8,256]{2,1,0:T(8,128)S(1)}, f32[5,8,256]{2,1,0:T(8,128)S(1)}, u32[]{:S(2)}, u32[]{:S(2)}) collective-permute-start(f32[5,8,256]{2,1,0:T(8,128)S(1)} %get-tuple-element.45), channel_id=1, source_target_pairs={{0,124},{4,0},{8,4},{12,8},{16,12},{20,16},{24,20},{28,24},{32,28}... | collective-permute-start | bytes 122888 | tf_op jit(solution)/shard_map/ppermute | solution.py:691
  14.8 1.7 %collective-permute-done.3.refs_3_.pack_back.refs_14_ = f32[5,8,256]{2,1,0:T(8,128)S(1)} collective-permute-done((f32[5,8,256]{2,1,0:T(8,128)S(1)}, f32[5,8,256]{2,1,0:T(8,128)S(1)}, u32[]{:S(2)}, u32[]{:S(2)}) %collective-permute-start.3) | collective-permute-done | bytes 40992 | tf_op jit(solution)/shard_map/ppermute | solution.py:691
  16.5 4.2 %collective-permute-start.5 = (f32[1,8,256]{2,1,0:T(8,128)S(1)}, f32[1,8,256]{2,1,0:T(8,128)S(1)}, u32[]{:S(2)}, u32[]{:S(2)}) collective-permute-start(f32[1,8,256]{2,1,0:T(8,128)S(1)} %get-tuple-element.47), channel_id=1, source_target_pairs={{0,16},{4,20},{8,24},{12,28},{16,32},{20,36},{24,40},{28,44},{32,4... | collective-permute-start | bytes 24584 | tf_op jit(solution)/shard_map/ppermute | solution.py:691
  20.7 2.1 %shard_map.73 = (f32[4,256,256]{2,1,0:T(8,128)S(1)}, f32[3,8,256]{2,1,0:T(8,128)S(1)}) custom-call(s32[1,4,16]{2,1,0:T(4,128)S(1)} %copy-done.3, f32[1,4,16]{2,1,0:T(4,128)S(1)} %copy-done.4), custom_call_target="tpu_custom_call" | custom-call | tf_op jit(solution)/shard_map/pallas_call | solution.py:536
  22.8 4.0 %collective-permute-done.1.pack2.refs_3_ = f32[6,8,256]{2,1,0:T(8,128)S(1)} collective-permute-done((f32[6,8,256]{2,1,0:T(8,128)S(1)}, f32[6,8,256]{2,1,0:T(8,128)S(1)}, u32[]{:S(2)}, u32[]{:S(2)}) %collective-permute-start.1) | collective-permute-done | bytes 49184 | tf_op jit(solution)/shard_map/ppermute | solution.py:691
  26.8 2.8 %collective-permute-done.pack1.refs_13_.refs_2_ = f32[10,8,256]{2,1,0:T(8,128)S(1)} collective-permute-done((f32[10,8,256]{2,1,0:T(8,128)S(1)}, f32[10,8,256]{2,1,0:T(8,128)S(1)}, u32[]{:S(2)}, u32[]{:S(2)}) %collective-permute-start) | collective-permute-done | bytes 81952 | tf_op jit(solution)/shard_map/ppermute | solution.py:691
  29.7 1.9 %collective-permute-start.10 = (f32[3,256,256]{2,1,0:T(8,128)S(1)}, f32[3,256,256]{2,1,0:T(8,128)S(1)}, u32[]{:S(2)}, u32[]{:S(2)}) collective-permute-start(f32[3,256,256]{2,1,0:T(8,128)S(1)} %get-tuple-element.67.refs_0_), channel_id=1, source_target_pairs={{0,24},{8,32},{16,40},{24,16},{32,56},{40,64},{48,72},{56,48},{64,... | collective-permute-start | bytes 2359304 | tf_op jit(solution)/shard_map/ppermute | solution.py:697
  31.6 0.4 collective-permute-start.9
  32.0 1.1 %shard_map.77 = (f32[8,8,256]{2,1,0:T(8,128)S(1)}, f32[6,8,256]{2,1,0:T(8,128)S(1)}, f32[16,8,256]{2,1,0:T(8,128)S(1)}, f32[16,8,256]{2,1,0:T(8,128)S(1)}, f32[8...) custom-call(s32[1,128]{1,0:T(1,128)S(1)} %copy-done.2, ...), custom_call_target="tpu_custom_call" | custom-call | tf_op jit(solution)/shard_map/pallas_call | solution.py:348
  33.0 0.6 %collective-permute-start.6 = (f32[12,8,256]{2,1,0:T(8,128)S(1)}, f32[12,8,256]{2,1,0:T(8,128)S(1)}, u32[]{:S(2)}, u32[]{:S(2)}) collective-permute-start(f32[12,8,256]{2,1,0:T(8,128)S(1)} %get-tuple-element.58.refs_15_), channel_id=1, source_target_pairs={{0,3},{1,0},{2,1},{3,2},{4,7},{5,4},{6,5},{7,6},{8,11},{9,8},{10,9... | collective-permute-start | bytes 294920 | tf_op jit(solution)/shard_map/ppermute | solution.py:691
  33.6 1.5 %collective-permute-start.7 = (f32[12,8,256]{2,1,0:T(8,128)S(1)}, f32[12,8,256]{2,1,0:T(8,128)S(1)}, u32[]{:S(2)}, u32[]{:S(2)}) collective-permute-start(f32[12,8,256]{2,1,0:T(8,128)S(1)} %get-tuple-element.59.refs_16_), channel_id=1, source_target_pairs={{0,1},{1,2},{2,3},{3,0},{4,5},{5,6},{6,7},{7,4},{8,9},{9,10},{10,1... | collective-permute-start | bytes 294920 | tf_op jit(solution)/shard_map/ppermute | solution.py:691
  35.1 3.1 %collective-permute-done.6.refs_17_ = f32[12,8,256]{2,1,0:T(8,128)S(1)} collective-permute-done((f32[12,8,256]{2,1,0:T(8,128)S(1)}, f32[12,8,256]{2,1,0:T(8,128)S(1)}, u32[]{:S(2)}, u32[]{:S(2)}) %collective-permute-start.6) | collective-permute-done | bytes 98336 | tf_op jit(solution)/shard_map/ppermute | solution.py:691
  38.2 0.9 %collective-permute-done.7.refs_18_ = f32[12,8,256]{2,1,0:T(8,128)S(1)} collective-permute-done((f32[12,8,256]{2,1,0:T(8,128)S(1)}, f32[12,8,256]{2,1,0:T(8,128)S(1)}, u32[]{:S(2)}, u32[]{:S(2)}) %collective-permute-start.7) | collective-permute-done | bytes 98336 | tf_op jit(solution)/shard_map/ppermute | solution.py:691
  39.1 5.4 %shard_map.78 = (f32[1,4,3,256,256]{4,3,2,1,0:T(8,128)}, f32[4,256,128]{2,1,0:T(8,128)S(1)}, f32[4,8,256]{2,1,0:T(8,128)S(1)}) custom-call(s32[1,128]{1,0:T(1,128)S(1)} %copy-done.2, s32[1,4,4]{2,1,0:T(4,128)S(1)} %copy-done.1, s32[1,4]{1,0:T(1,128)S(1)} %copy-done.5, f32[3,8,256]{2,1,0:T(8,128)S(1)} %get-tuple-element.37.edge_spill.refs_2_.refs_7_, ...), custom_call_target="tpu_custom_call" | custom-call | tf_op jit(solution)/shard_map/pallas_call | solution.py:646
  44.5 1.2 %collective-permute-done.10.refs_1_ = f32[3,256,256]{2,1,0:T(8,128)S(1)} collective-permute-done((f32[3,256,256]{2,1,0:T(8,128)S(1)}, f32[3,256,256]{2,1,0:T(8,128)S(1)}, u32[]{:S(2)}, u32[]{:S(2)}) %collective-permute-start.10) | collective-permute-done | bytes 786464 | tf_op jit(solution)/shard_map/ppermute | solution.py:697
  45.7 3.2 %shard_map.80.refs_1_ = f32[1,4,3,256,256]{4,3,2,1,0:T(8,128)} custom-call(s32[1,128]{1,0:T(1,128)S(1)} %copy-done.2, s32[1,4]{1,0:T(1,128)S(1)} %copy-done.5, f32[1,4,2,256,256]{4,3,2,1,0:T(8,128)S(1)} %copy-done, f32[4,256,128]{2,1,0:T(8,128)S(1)} %get-tuple-element.62.columns, ...), custom_call_target="tpu_custom_call", output_to_operand_aliasing={{}: (8, {})} | custom-call | tf_op jit(solution)/shard_map/pallas_call | solution.py:677
  48.9 5.2 %collective-permute-done.9.refs_0_ = f32[3,256,256]{2,1,0:T(8,128)S(1)} collective-permute-done((f32[3,256,256]{2,1,0:T(8,128)S(1)}, f32[3,256,256]{2,1,0:T(8,128)S(1)}, u32[]{:S(2)}, u32[]{:S(2)}) %collective-permute-start.9) | collective-permute-done | bytes 786464 | tf_op jit(solution)/shard_map/ppermute | solution.py:697
  54.1 3.0 %shard_map.81 = f32[1,4,3,256,256]{4,3,2,1,0:T(8,128)} custom-call(s32[1,128]{1,0:T(1,128)S(1)} %copy-done.2, s32[1,4]{1,0:T(1,128)S(1)} %copy-done.5, f32[1,4,2,256,256]{4,3,2,1,0:T(8,128)S(1)} %copy-done, f32[4,256,128]{2,1,0:T(8,128)S(1)} %get-tuple-element.62.columns, f32[4,8,256]{2,1,0:T(8,128)S(1)} %get-tuple-element.63.rows, ...), custom_call_target="tpu_custom_call", output_to_operand_aliasing={{}: (7, {})} | custom-call | tf_op jit(solution)/shard_map/pallas_call | solution.py:677
  (19 shorter events, 0.1 us)
Async XLA Ops:
  2.1 14.4 %collective-permute-start.2 = (f32[3,256,256]{2,1,0:T(8,128)S(1)}, f32[3,256,256]{2,1,0:T(8,128)S(1)}, u32[]{:S(2)}, u32[]{:S(2)}) collective-permute-start(f32[3,256,256]{2,1,0:T(8,128)S(1)} %get-tuple-element.39.block_w), channel_id=1, source_target_pairs={{0,4},{4,24},{8,12},{12,0},{16,20},{20,8},{24,28},{28,16},{32,36},... | collective-permute-start | bytes 2359304 | tf_op jit(solution)/shard_map/ppermute | solution.py:697
  2.2 18.5 %copy-start.3 = (s32[1,4,16]{2,1,0:T(4,128)S(1)}, s32[1,4,16]{2,1,0:T(4,128)}, u32[]{:S(2)}) copy-start(s32[1,4,16]{2,1,0:T(4,128)} %cells.3) | copy-start | bytes 772
  2.2 18.5 %copy-start.4 = (f32[1,4,16]{2,1,0:T(4,128)S(1)}, f32[1,4,16]{2,1,0:T(4,128)}, u32[]{:S(2)}) copy-start(f32[1,4,16]{2,1,0:T(4,128)} %rates.3) | copy-start | bytes 772
  2.2 27.4 %collective-permute-start.8 = (f32[3,256,256]{2,1,0:T(8,128)S(1)}, f32[3,256,256]{2,1,0:T(8,128)S(1)}, u32[]{:S(2)}, u32[]{:S(2)}) collective-permute-start(f32[3,256,256]{2,1,0:T(8,128)S(1)} %get-tuple-element.38.block_a), channel_id=1, source_target_pairs={{0,8},{4,12},{8,16},{12,20},{16,24},{20,28},{24,32},{28,36},{32,40... | collective-permute-start | bytes 2359304 | tf_op jit(solution)/shard_map/ppermute | solution.py:691
  7.9 24.1 %copy-start.1 = (s32[1,4,4]{2,1,0:T(4,128)S(1)}, s32[1,4,4]{2,1,0:T(4,128)}, u32[]{:S(2)}) copy-start(s32[1,4,4]{2,1,0:T(4,128)} %refs_0_.1) | copy-start | bytes 196
  7.9 24.1 %copy-start.2 = (s32[1,128]{1,0:T(1,128)S(1)}, s32[1,128]{1,0:T(1,128)}, u32[]{:S(2)}) copy-start(s32[1,128]{1,0:T(1,128)} %dest.11) | copy-start | bytes 1540
  7.9 31.2 %copy-start = (f32[1,4,2,256,256]{4,3,2,1,0:T(8,128)S(1)}, f32[1,4,2,256,256]{4,3,2,1,0:T(8,128)}, u32[]{:S(2)}) copy-start(f32[1,4,2,256,256]{4,3,2,1,0:T(8,128)} %terrain.3) | copy-start | bytes 6291460
  7.9 31.2 %copy-start.5 = (s32[1,4]{1,0:T(1,128)S(1)}, s32[1,4]{1,0:T(1,128)}, u32[]{:S(2)}) copy-start(s32[1,4]{1,0:T(1,128)} %wet.3) | copy-start | bytes 52
  7.9 8.6 %collective-permute-start.3 = (f32[5,8,256]{2,1,0:T(8,128)S(1)}, f32[5,8,256]{2,1,0:T(8,128)S(1)}, u32[]{:S(2)}, u32[]{:S(2)}) collective-permute-start(f32[5,8,256]{2,1,0:T(8,128)S(1)} %get-tuple-element.45), channel_id=1, source_target_pairs={{0,124},{4,0},{8,4},{12,8},{16,12},{20,16},{24,20},{28,24},{32,28}... | collective-permute-start | bytes 122888 | tf_op jit(solution)/shard_map/ppermute | solution.py:691
  14.8 14.8 %collective-permute-start = (f32[10,8,256]{2,1,0:T(8,128)S(1)}, f32[10,8,256]{2,1,0:T(8,128)S(1)}, u32[]{:S(2)}, u32[]{:S(2)}) collective-permute-start(f32[10,8,256]{2,1,0:T(8,128)S(1)} %get-tuple-element.41), channel_id=1, source_target_pairs={{0,4},{4,8},{8,12},{12,16},{16,20},{20,24},{24,28},{28,32},{32,36}... | collective-permute-start | bytes 245768 | tf_op jit(solution)/shard_map/ppermute | solution.py:691
  14.8 12.0 %collective-permute-start.1 = (f32[6,8,256]{2,1,0:T(8,128)S(1)}, f32[6,8,256]{2,1,0:T(8,128)S(1)}, u32[]{:S(2)}, u32[]{:S(2)}) collective-permute-start(f32[6,8,256]{2,1,0:T(8,128)S(1)} %get-tuple-element.42), channel_id=1, source_target_pairs={{0,8},{4,12},{8,16},{12,20},{16,24},{20,28},{24,32},{28,36},{32,40... | collective-permute-start | bytes 147464 | tf_op jit(solution)/shard_map/ppermute | solution.py:691
  16.5 13.2 %collective-permute-start.4 = (f32[5,8,256]{2,1,0:T(8,128)S(1)}, f32[5,8,256]{2,1,0:T(8,128)S(1)}, u32[]{:S(2)}, u32[]{:S(2)}) collective-permute-start(f32[5,8,256]{2,1,0:T(8,128)S(1)} %get-tuple-element.46), channel_id=1, source_target_pairs={{0,12},{4,16},{8,20},{12,24},{16,28},{20,32},{24,36},{28,40},{32,4... | collective-permute-start | bytes 122888 | tf_op jit(solution)/shard_map/ppermute | solution.py:691
  16.5 13.2 %collective-permute-start.5 = (f32[1,8,256]{2,1,0:T(8,128)S(1)}, f32[1,8,256]{2,1,0:T(8,128)S(1)}, u32[]{:S(2)}, u32[]{:S(2)}) collective-permute-start(f32[1,8,256]{2,1,0:T(8,128)S(1)} %get-tuple-element.47), channel_id=1, source_target_pairs={{0,16},{4,20},{8,24},{12,28},{16,32},{20,36},{24,40},{28,44},{32,4... | collective-permute-start | bytes 24584 | tf_op jit(solution)/shard_map/ppermute | solution.py:691
  29.7 16.0 %collective-permute-start.10 = (f32[3,256,256]{2,1,0:T(8,128)S(1)}, f32[3,256,256]{2,1,0:T(8,128)S(1)}, u32[]{:S(2)}, u32[]{:S(2)}) collective-permute-start(f32[3,256,256]{2,1,0:T(8,128)S(1)} %get-tuple-element.67.refs_0_), channel_id=1, source_target_pairs={{0,24},{8,32},{16,40},{24,16},{32,56},{40,64},{48,72},{56,48},{64,... | collective-permute-start | bytes 2359304 | tf_op jit(solution)/shard_map/ppermute | solution.py:697
  31.6 22.6 %collective-permute-start.9 = (f32[3,256,256]{2,1,0:T(8,128)S(1)}, f32[3,256,256]{2,1,0:T(8,128)S(1)}, u32[]{:S(2)}, u32[]{:S(2)}) collective-permute-start(f32[3,256,256]{2,1,0:T(8,128)S(1)} %get-tuple-element.66), channel_id=1, source_target_pairs={{0,12},{4,8},{8,20},{12,16},{16,28},{20,24},{24,36},{28,32},{32,44... | collective-permute-start | bytes 2359304 | tf_op jit(solution)/shard_map/ppermute | solution.py:697
  33.0 5.2 %collective-permute-start.6 = (f32[12,8,256]{2,1,0:T(8,128)S(1)}, f32[12,8,256]{2,1,0:T(8,128)S(1)}, u32[]{:S(2)}, u32[]{:S(2)}) collective-permute-start(f32[12,8,256]{2,1,0:T(8,128)S(1)} %get-tuple-element.58.refs_15_), channel_id=1, source_target_pairs={{0,3},{1,0},{2,1},{3,2},{4,7},{5,4},{6,5},{7,6},{8,11},{9,8},{10,9... | collective-permute-start | bytes 294920 | tf_op jit(solution)/shard_map/ppermute | solution.py:691
  33.6 5.4 %collective-permute-start.7 = (f32[12,8,256]{2,1,0:T(8,128)S(1)}, f32[12,8,256]{2,1,0:T(8,128)S(1)}, u32[]{:S(2)}, u32[]{:S(2)}) collective-permute-start(f32[12,8,256]{2,1,0:T(8,128)S(1)} %get-tuple-element.59.refs_16_), channel_id=1, source_target_pairs={{0,1},{1,2},{2,3},{3,0},{4,5},{5,6},{6,7},{7,4},{8,9},{9,10},{10,1... | collective-permute-start | bytes 294920 | tf_op jit(solution)/shard_map/ppermute | solution.py:691
